TPU v7x, 256 devices: a whole 4x4x8 slice. The times are simulated.
256 devices in a mesh: dom: 16 (over z, core), head: 16 (over x, y).
Axes of the slice: x: 4, y: 4, z: 8, core: 2. Of those that a mesh axis runs over, the one named last changes fastest.
Arguments:
- features: bfloat16 [32768, 1024], P(('dom', 'head')), as said below
- w_query: bfloat16 [1024, 1024], P(None, 'head'), as said below
- w_key: bfloat16 [1024, 1024], P(None, 'head'), as said below
- w_value: bfloat16 [1024, 1024], P(None, 'head'), may hold values from -0.1875 to 0.1875
- w_output: bfloat16 [1024, 1024], P('head'), may hold values from -0.1875 to 0.1875
- cotangent: bfloat16 [32768, 1024], P(('dom', 'head')), may hold values from -24 to 24
- cross_source: int32 [16, 16], P('dom'), may hold values from 0 to 255, as said below
- cross_target: int32 [16, 16], P('dom'), may hold values from 0 to 15, as said below
- cross_count: int32 [16], P('dom'), may hold values from 12 to 16, as said below
Outputs:
- layer_out: bfloat16 [32768, 1024], P(('dom', 'head'))
- grad_features: bfloat16 [32768, 1024], P(('dom', 'head'))
- w_query_grad: float32 [1024, 1024], P('dom', 'head')
- w_key_grad: float32 [1024, 1024], P('dom', 'head')
- w_value_grad: float32 [1024, 1024], P('dom', 'head')
- w_output_grad_t: float32 [1024, 1024], P('dom', 'head')
Inputs may be any that keep to these rules, and one draw needn't show every extreme that they name: `cross_source`: row p names global blocks of partitions other than p; at most 2 entries of one row lie in any one partition, and some row has exactly 2 in one partition. `cross_target`: the entries of one row are distinct. `cross_count`: some partition has 16 live slots. `features`: entries lie within 10 in magnitude. `w_query`: entries lie within 5 / sqrt(1024) in magnitude. `w_key`: entries lie within 5 / sqrt(1024) in magnitude.
All inputs are finite; a program needn't handle non-finite values.
Results may differ from a plain program's by a relative error of at most 0.018.
Values may be sent and summed in bfloat16 or wider, within the bound.
A program may use at most 64 MiB of HBM per device.

v0:
```python
import math

import jax
import jax.numpy as jnp
from jax import lax
from jax.sharding import PartitionSpec as P

HD = 64
BLK = 128
CAP = 2


NEG_FILL = -1e30


def contract_rows(left, right):
    return lax.dot_general(
        left, right, (((0,), (0,)), ((), ())), preferred_element_type=jnp.float32
    )


def contract_cols(left, right):
    return lax.dot_general(
        left, right, (((1,), (1,)), ((), ())), preferred_element_type=jnp.float32
    )


def block_probs(query_grp, key_head, extra_keys, usable, scaling):
    local_scores = (
        jnp.einsum("gbd,nd->gbn", query_grp, key_head, preferred_element_type=jnp.float32) * scaling
    )
    extra_scores = (
        jnp.einsum("gbd,ged->gbe", query_grp, extra_keys, preferred_element_type=jnp.float32)
        * scaling
    )
    extra_scores = jnp.where(usable[:, None, None], extra_scores, NEG_FILL)
    highest = jnp.maximum(jnp.max(local_scores, -1), jnp.max(extra_scores, -1))[..., None]
    local_exp = jnp.exp(local_scores - highest)
    extra_exp = jnp.exp(extra_scores - highest)
    denominator = jnp.sum(local_exp, -1, keepdims=True) + jnp.sum(extra_exp, -1, keepdims=True)
    return (local_exp / denominator, extra_exp / denominator)


def head_forward(queries, keys, values, extra_keys, extra_values, usable, group_size, scaling):
    node_total, head_cols = queries.shape
    groups = node_total // (group_size * BLK)
    shape_four = (groups, group_size, BLK, head_cols)

    def one_group(inputs):
        query_grp, extra_k, extra_v, usable_grp = inputs
        local_probs, extra_probs = block_probs(query_grp, keys, extra_k, usable_grp, scaling)
        result = jnp.einsum(
            "gbn,nd->gbd",
            local_probs.astype(jnp.bfloat16),
            values,
            preferred_element_type=jnp.float32,
        )
        result = result + jnp.einsum(
            "gbe,ged->gbd",
            extra_probs.astype(jnp.bfloat16),
            extra_v,
            preferred_element_type=jnp.float32,
        )
        return result.astype(jnp.bfloat16)

    result = lax.map(
        one_group,
        (
            queries.reshape(shape_four),
            extra_keys.reshape(shape_four),
            extra_values.reshape(shape_four),
            usable.reshape(groups, group_size),
        ),
    )
    return result.reshape(node_total, head_cols)


def head_backward(
    queries,
    keys,
    values,
    extra_keys,
    extra_values,
    usable,
    attended,
    grad_attended,
    group_size,
    scaling,
):
    node_total, head_cols = queries.shape
    groups = node_total // (group_size * BLK)
    shape_four = (groups, group_size, BLK, head_cols)

    def one_group(carried, inputs):
        key_acc, value_acc = carried
        query_grp, extra_k, extra_v, usable_grp, out_grp, dout_grp = inputs
        local_probs, extra_probs = block_probs(query_grp, keys, extra_k, usable_grp, scaling)
        local_bf = local_probs.astype(jnp.bfloat16)
        extra_bf = extra_probs.astype(jnp.bfloat16)
        row_delta = jnp.sum(dout_grp.astype(jnp.float32) * out_grp.astype(jnp.float32), -1)[
            ..., None
        ]
        local_dprob = jnp.einsum(
            "gbd,nd->gbn", dout_grp, values, preferred_element_type=jnp.float32
        )
        extra_dprob = jnp.einsum(
            "gbd,ged->gbe", dout_grp, extra_v, preferred_element_type=jnp.float32
        )
        local_dscore = (local_probs * (local_dprob - row_delta) * scaling).astype(jnp.bfloat16)
        extra_dscore = (extra_probs * (extra_dprob - row_delta) * scaling).astype(jnp.bfloat16)
        grad_query = jnp.einsum(
            "gbn,nd->gbd", local_dscore, keys, preferred_element_type=jnp.float32
        )
        grad_query = grad_query + jnp.einsum(
            "gbe,ged->gbd", extra_dscore, extra_k, preferred_element_type=jnp.float32
        )
        key_acc = key_acc + jnp.einsum(
            "gbn,gbd->nd", local_dscore, query_grp, preferred_element_type=jnp.float32
        )
        value_acc = value_acc + jnp.einsum(
            "gbn,gbd->nd", local_bf, dout_grp, preferred_element_type=jnp.float32
        )
        extra_dkey = jnp.einsum(
            "gbe,gbd->ged", extra_dscore, query_grp, preferred_element_type=jnp.float32
        )
        extra_dvalue = jnp.einsum(
            "gbe,gbd->ged", extra_bf, dout_grp, preferred_element_type=jnp.float32
        )
        return ((key_acc, value_acc), (grad_query.astype(jnp.bfloat16), extra_dkey, extra_dvalue))

    zero_acc = jnp.zeros((node_total, head_cols), jnp.float32)
    carried, stacked = lax.scan(
        one_group,
        (zero_acc, zero_acc),
        (
            queries.reshape(shape_four),
            extra_keys.reshape(shape_four),
            extra_values.reshape(shape_four),
            usable.reshape(groups, group_size),
            attended.reshape(shape_four),
            grad_attended.reshape(shape_four),
        ),
    )
    grad_query, extra_dkey, extra_dvalue = stacked
    return (
        grad_query.reshape(node_total, head_cols),
        carried[0],
        carried[1],
        extra_dkey.reshape(node_total, head_cols),
        extra_dvalue.reshape(node_total, head_cols),
    )


def local(
    features, w_query, w_key, w_value, w_output, cotangent, cross_source, cross_target, cross_count
):
    part_total = lax.axis_size("dom")
    columns = w_query.shape[1]
    scaling = 1.0 / math.sqrt(HD)
    part_rows = lax.all_gather(features, "head", axis=0, tiled=True)
    part_cot = lax.all_gather(cotangent, "head", axis=0, tiled=True)
    node_total = part_rows.shape[0]
    blocks = node_total // BLK
    group_size = math.gcd(blocks, 4)
    w_joined = jnp.concatenate([w_query, w_key, w_value], 1)
    projected = jnp.dot(part_rows, w_joined, preferred_element_type=jnp.float32).astype(
        jnp.bfloat16
    )
    queries = projected[:, :columns]
    keys = projected[:, columns : 2 * columns]
    values = projected[:, 2 * columns :]
    source = cross_source[0]
    target = cross_target[0]
    live_count = cross_count[0]
    slot_total = source.shape[0]
    owners = source // blocks
    block_local = source % blocks
    slot_ids = jnp.arange(slot_total, dtype=jnp.int32)
    earlier = (owners[:, None] == owners[None, :]) & (slot_ids[None, :] < slot_ids[:, None])
    position = jnp.sum(earlier.astype(jnp.int32), 1)
    placed = (owners[:, None, None] == jnp.arange(part_total, dtype=jnp.int32)[None, :, None]) & (
        position[:, None, None] == jnp.arange(CAP, dtype=jnp.int32)[None, None, :]
    )
    request = jnp.sum(jnp.where(placed, block_local[:, None, None], 0), 0)
    asked_blocks = lax.all_to_all(request, "dom", split_axis=0, concat_axis=0, tiled=True)
    key_value = jnp.concatenate([keys, values], 1).reshape(blocks, BLK, 2 * columns)
    outgoing = jnp.take(key_value, asked_blocks.reshape(-1), axis=0).reshape(
        part_total, CAP, BLK, 2 * columns
    )
    incoming = lax.all_to_all(outgoing, "dom", split_axis=0, concat_axis=0, tiled=True)
    slot_blocks = jnp.take(
        incoming.reshape(part_total * CAP, BLK, 2 * columns), owners * CAP + position, axis=0
    )
    chosen = (target[None, :] == jnp.arange(blocks, dtype=jnp.int32)[:, None]) & (
        slot_ids < live_count
    )[None, :]
    extra_rows = jnp.einsum(
        "tj,jbc->tbc", chosen.astype(jnp.bfloat16), slot_blocks, preferred_element_type=jnp.float32
    ).astype(jnp.bfloat16)
    usable = jnp.any(chosen, 1)

    def extra_head(head_index, offset):
        low = offset + head_index * HD
        return extra_rows[:, :, low : low + HD].reshape(node_total, HD)

    head_index = 0
    low = head_index * HD
    outputs = head_forward(
        queries,
        keys,
        values,
        extra_head(head_index, 0),
        extra_head(head_index, columns),
        usable,
        group_size,
        scaling,
    )
    merged = lax.psum_scatter(
        jnp.dot(outputs, w_output, preferred_element_type=jnp.float32).astype(jnp.bfloat16),
        "head",
        scatter_dimension=0,
        tiled=True,
    ).astype(jnp.float32)
    layer_out = (features.astype(jnp.float32) + merged).astype(jnp.bfloat16)
    grad_attended = contract_cols(part_cot, w_output).astype(jnp.bfloat16)
    grad_q_list, key_list, value_list, dkey_list, dvalue_list = ([], [], [], [], [])
    head_index = 0
    low = head_index * HD
    pieces = head_backward(
        queries,
        keys,
        values,
        extra_head(head_index, 0),
        extra_head(head_index, columns),
        usable,
        outputs,
        grad_attended,
        group_size,
        scaling,
    )
    grad_q_list.append(pieces[0])
    key_list.append(pieces[1])
    value_list.append(pieces[2])
    dkey_list.append(pieces[3])
    dvalue_list.append(pieces[4])
    grad_queries = grad_q_list[0]
    key_local = key_list[0]
    value_local = value_list[0]
    extra_grad = jnp.concatenate(dkey_list + dvalue_list, 1).reshape(blocks, BLK, 2 * columns)
    slot_grad = jnp.einsum(
        "tj,tbc->jbc", chosen.astype(jnp.float32), extra_grad, precision=lax.Precision.HIGHEST
    )
    sending = jnp.einsum(
        "jpr,jbc->prbc", placed.astype(jnp.float32), slot_grad, precision=lax.Precision.HIGHEST
    )
    returned = lax.all_to_all(
        sending.astype(jnp.bfloat16), "dom", split_axis=0, concat_axis=0, tiled=True
    ).astype(sending.dtype)
    owner_hit = (
        asked_blocks.reshape(-1)[:, None] == jnp.arange(blocks, dtype=jnp.int32)[None, :]
    ).astype(jnp.float32)
    received = jnp.einsum(
        "rt,rbc->tbc",
        owner_hit,
        returned.reshape(part_total * CAP, BLK, 2 * columns),
        precision=lax.Precision.HIGHEST,
    ).reshape(node_total, 2 * columns)
    grad_keys = (key_local + received[:, :columns]).astype(jnp.bfloat16)
    grad_values = (value_local + received[:, columns:]).astype(jnp.bfloat16)
    grad_joined = jnp.concatenate([grad_queries, grad_keys, grad_values], 1)
    weight_sums = lax.psum_scatter(
        jnp.concatenate(
            [contract_rows(part_rows, grad_joined), contract_rows(part_cot, outputs)], 1
        ).astype(jnp.bfloat16),
        "dom",
        scatter_dimension=0,
        tiled=True,
    ).astype(jnp.float32)
    back_sum = lax.psum_scatter(
        contract_cols(grad_joined, w_joined).astype(jnp.bfloat16),
        "head",
        scatter_dimension=0,
        tiled=True,
    ).astype(jnp.float32)
    grad_features = (cotangent.astype(jnp.float32) + back_sum).astype(jnp.bfloat16)
    return (
        layer_out,
        grad_features,
        weight_sums[:, :columns],
        weight_sums[:, columns : 2 * columns],
        weight_sums[:, 2 * columns : 3 * columns],
        weight_sums[:, 3 * columns :],
    )


def solution(mesh):
    return jax.shard_map(
        local,
        mesh=mesh,
        in_specs=(
            P(("dom", "head"), None),
            P(None, "head"),
            P(None, "head"),
            P(None, "head"),
            P("head", None),
            P(("dom", "head"), None),
            P("dom", None),
            P("dom", None),
            P("dom"),
        ),
        out_specs=(
            P(("dom", "head"), None),
            P(("dom", "head"), None),
            P("dom", "head"),
            P("dom", "head"),
            P("dom", "head"),
            P("dom", "head"),
        ),
        check_vma=False,
    )
```

profile of v0, /device:TPU:1, one launch (start us, length us, event | category | flops | bytes accessed | tf_op | source)
XLA Modules:
  0.0 474.3 jit_solution(4540939554119667517)
XLA Ops:
  10.9 10.0 %all-to-all-start = ((s32[16,1,2]{2,1,0:T(1,128)}), s32[16,1,2]{2,1,0:T(1,128)S(1)}, u32[]{:S(2)}, u32[]{:S(2)}) async-start(s32[16,1,2]{2,1,0:T(1,128)} %copy.67), calls=%async_computation | async-start | bytes 16384 | tf_op jit(solution)/shard_map/all_to_all | solution.py:185
  23.7 4.2 all-to-all-done
  29.3 41.5 %all-gather.3.cloned.1.call-done = bf16[2048,1024]{1,0:T(8,128)(2,1)} async-done(((bf16[128,1024]{1,0:T(8,128)(2,1)}), bf16[2048,1024]{1,0:T(8,128)(2,1)}) %all-gather.3.cloned.1.call-update) | async-done | bytes 4194320 | tf_op jit(solution)/shard_map/all_gather | solution.py:160
  70.8 3.7 fusion.70
  75.7 1.2 broadcast_select_fusion
  76.9 7.7 %all-to-all-start.1 = ((bf16[16,2,128,128]{3,2,1,0:T(8,128)(2,1)}), bf16[16,2,128,128]{3,2,1,0:T(8,128)(2,1)S(1)}, u32[]{:S(2)}, u32[]{:S(2)}) async-start(bf16[16,2,128,128]{3,2,1,0:T(8,128)(2,1)} %broadcast_select_fusion), calls=%async_computation.1 | async-start | bytes 2097152 | tf_op jit(solution)/shard_map/all_to_all | solution.py:190
  86.6 43.0 %all-gather.5.cloned.1.call-done = bf16[2048,1024]{1,0:T(8,128)(2,1)} async-done(((bf16[128,1024]{1,0:T(8,128)(2,1)}), bf16[2048,1024]{1,0:T(8,128)(2,1)}) %all-gather.5.cloned.1.call-update) | async-done | bytes 4194320 | tf_op jit(solution)/shard_map/all_gather | solution.py:161
  129.6 3.6 convolution_convert_fusion.3
  135.8 1.2 convolution_convert_fusion.5
  137.2 1.2 copy.75
  138.8 20.3 %while.29 = (s32[]{:T(128)}, bf16[4,4,128,64]{2,3,1,0:T(8,128)(2,1)S(1)}, bf16[4,4,128,64]{2,3,1,0:T(8,128)(2,1)S(1)}, bf16[2048,64]{0,1:T(8,128)(2,1)S(1)}, pre...) while((s32[]{:T(128)}, ...), condition=%wide.region_8.9_spmd, body=%wide.region_3.8_spmd.sunk | while | flops 295238656 | bytes 15567505 | solution.py:66
  141.6 1.3 fusion.158
  142.9 1.0 fusion.159
  146.7 1.3 fusion.158
  148.0 1.0 fusion.159
  151.7 1.3 fusion.158
  153.0 1.0 fusion.159
  156.8 1.3 fusion.158
  158.1 1.0 fusion.159
  159.2 36.6 %while.30 = (s32[]{:T(128)}, f32[2048,64]{0,1:T(8,128)S(1)}, f32[2048,64]{0,1:T(8,128)S(1)}, bf16[4,4,128,64]{2,1,0,3:T(4,128)(2,1)}, f32[4,4,128,64]{2,3,1,0:T(...) while((s32[]{:T(128)}, f32[2048,64]{0,1:T(8,128)S(1)}, ...), condition=%wide.region_16.17_spmd.clone, body=%wide.region_10.16_spmd.clone.sunk | while | flops 731445760 | bytes 30196460 | solution.py:132
  161.9 1.1 fusion.179
  163.6 1.2 fusion.178
  164.7 1.6 multiply_convert_fusion.2
  171.1 1.1 fusion.179
  172.7 1.2 fusion.178
  173.9 1.6 multiply_convert_fusion.2
  180.2 1.1 fusion.179
  181.8 1.2 fusion.178
  183.0 1.6 multiply_convert_fusion.2
  189.3 1.1 fusion.179
  191.0 1.2 fusion.178
  192.2 1.6 multiply_convert_fusion.2
  197.2 1.4 convolution_bitcast_fusion.4
  198.6 1.7 convolution_convert_fusion.4
  200.3 1.3 copy.84
  201.6 7.7 %all-to-all-start.2 = ((bf16[16,2,128,128]{3,2,1,0:T(8,128)(2,1)}), bf16[16,2,128,128]{3,2,1,0:T(8,128)(2,1)S(1)}, u32[]{:S(2)}, u32[]{:S(2)}) async-start(bf16[16,2,128,128]{3,2,1,0:T(8,128)(2,1)} %copy.84), calls=%async_computation.3 | async-start | bytes 2097152 | tf_op jit(solution)/shard_map/all_to_all | solution.py:256
  210.7 3.7 fusion.72
  214.4 22.8 %all-to-all-done.2 = bf16[16,2,128,128]{3,2,1,0:T(8,128)(2,1)S(1)} async-done(((bf16[16,2,128,128]{3,2,1,0:T(8,128)(2,1)}), bf16[16,2,128,128]{3,2,1,0:T(8,128)(2,1)S(1)}, u32[]{:S(2)}, u32[]{:S(2)}) %all-to-all-start.2) | async-done | bytes 1048608 | tf_op jit(solution)/shard_map/all_to_all | solution.py:256
  239.3 1.2 add_convert_fusion.1
  240.5 3.2 fusion.71
  243.7 1.1 copy.102
  244.8 3.2 convolution_convert_fusion.1
  248.1 3.3 convolution_convert_fusion
  251.4 42.7 %reduce-scatter.10.cloned.1.call-done = bf16[64,256]{1,0:T(8,128)(2,1)} async-done(((bf16[1024,256]{1,0:T(8,128)(2,1)}), bf16[64,256]{1,0:T(8,128)(2,1)}) %reduce-scatter.10.cloned.1.call-update) | async-done | bytes 32784
  297.8 82.6 %reduce-scatter.6.cloned.1.call-done = bf16[128,1024]{1,0:T(8,128)(2,1)} async-done(((bf16[2048,1024]{1,0:T(8,128)(2,1)}), bf16[128,1024]{1,0:T(8,128)(2,1)}) %reduce-scatter.6.cloned.1.call-update) | async-done | bytes 262160 | tf_op jit(solution)/shard_map/reduce_scatter | solution.py:218
  380.4 1.7 add_convert_fusion.3
  382.1 83.9 %reduce-scatter.8.cloned.1.call-done = bf16[128,1024]{1,0:T(8,128)(2,1)} async-done(((bf16[2048,1024]{1,0:T(8,128)(2,1)}), bf16[128,1024]{1,0:T(8,128)(2,1)}) %reduce-scatter.8.cloned.1.call-update) | async-done | bytes 262160 | tf_op jit(solution)/shard_map/reduce_scatter | solution.py:279
  466.0 1.7 add_convert_fusion
  (208 shorter events, 53.9 us)
Async XLA Ops:
  7.2 122.4 %copy-start = (bf16[64,1024]{1,0:T(8,128)(2,1)S(1)}, bf16[64,1024]{1,0:T(8,128)(2,1)}, u32[]{:S(2)}) copy-start(bf16[64,1024]{1,0:T(8,128)(2,1)} %param.17) | copy-start | bytes 393220
  7.2 63.6 %all-gather.3.cloned.1.call-start = ((), (), s32[]{:S(2)}) async-start(), calls=%async_computation.6 | async-start | bytes 4456448 | tf_op jit(solution)/shard_map/all_gather | solution.py:160
  7.9 121.7 %all-gather.5.cloned.1.call-start = ((), (), s32[]{:S(2)}) async-start(), calls=%async_computation.8 | async-start | bytes 4456448 | tf_op jit(solution)/shard_map/all_gather | solution.py:161
  10.1 0.8 copy-start.17
  10.9 16.9 %all-to-all-start = ((s32[16,1,2]{2,1,0:T(1,128)}), s32[16,1,2]{2,1,0:T(1,128)S(1)}, u32[]{:S(2)}, u32[]{:S(2)}) async-start(s32[16,1,2]{2,1,0:T(1,128)} %copy.67), calls=%async_computation | async-start | bytes 16384 | tf_op jit(solution)/shard_map/all_to_all | solution.py:185
  23.7 50.9 %copy-start.3 = (bf16[1024,192]{0,1:T(8,128)(2,1)}, bf16[1024,192]{0,1:T(8,128)(2,1)S(1)}, u32[]{:S(2)}) copy-start(bf16[1024,192]{0,1:T(8,128)(2,1)S(1)} %constant_dynamic-update-slice_fusion) | copy-start | bytes 1179652
  74.6 10.7 %copy-start.14 = (s32[1,16]{1,0:T(1,128)S(1)}, s32[1,16]{1,0:T(1,128)}, u32[]{:S(2)}) copy-start(s32[1,16]{1,0:T(1,128)} %param.20) | copy-start | bytes 196
  74.6 11.4 %copy-start.18 = (s32[1,16]{1,0:T(1,128)S(1)}, s32[1,16]{1,0:T(1,128)}, u32[]{:S(2)}) copy-start(s32[1,16]{1,0:T(1,128)} %param.19) | copy-start | bytes 196
  76.9 57.5 %all-to-all-start.1 = ((bf16[16,2,128,128]{3,2,1,0:T(8,128)(2,1)}), bf16[16,2,128,128]{3,2,1,0:T(8,128)(2,1)S(1)}, u32[]{:S(2)}, u32[]{:S(2)}) async-start(bf16[16,2,128,128]{3,2,1,0:T(8,128)(2,1)} %broadcast_select_fusion), calls=%async_computation.1 | async-start | bytes 2097152 | tf_op jit(solution)/shard_map/all_to_all | solution.py:190
  85.3 1.3 copy-start.16
  138.8 20.3 %copy-start.5 = (f32[4,4,128,64]{2,3,1,0:T(8,128)S(1)}, f32[4,4,128,64]{2,3,1,0:T(8,128)}, u32[]{:S(2)}) copy-start(f32[4,4,128,64]{2,3,1,0:T(8,128)} %custom-call.10) | copy-start | bytes 1572868
  138.8 20.3 %copy-start.6 = (f32[4,4,128,64]{2,3,1,0:T(8,128)S(1)}, f32[4,4,128,64]{2,3,1,0:T(8,128)}, u32[]{:S(2)}) copy-start(f32[4,4,128,64]{2,3,1,0:T(8,128)} %custom-call.9) | copy-start | bytes 1572868
  138.8 20.3 %copy-start.7 = (f32[2048,64]{0,1:T(8,128)S(1)}, f32[2048,64]{0,1:T(8,128)}, u32[]{:S(2)}) copy-start(f32[2048,64]{0,1:T(8,128)} %custom-call.1) | copy-start | bytes 1572868
  139.9 1.7 copy-start.12
  144.9 1.7 copy-start.12
  150.0 1.7 copy-start.12
  155.0 1.7 copy-start.12
  159.2 38.0 %copy-start.15 = (s32[1,16]{1,0:T(1,128)S(1)}, s32[1,16]{1,0:T(1,128)}, u32[]{:S(2)}) copy-start(s32[1,16]{1,0:T(1,128)} %param.20) | copy-start | bytes 196
  163.6 1.2 copy-start.13
  172.7 1.2 copy-start.13
  181.8 1.2 copy-start.13
  191.0 1.2 copy-start.13
  195.8 0.8 copy-start.8
  198.6 11.1 %copy-start.10 = (bf16[4,4,128,64]{2,1,0,3:T(4,128)(2,1)S(1)}, bf16[4,4,128,64]{2,1,0,3:T(4,128)(2,1)}, u32[]{:S(2)}) copy-start(bf16[4,4,128,64]{2,1,0,3:T(4,128)(2,1)} %get-tuple-element.125) | copy-start | bytes 786436
  201.6 35.6 %all-to-all-start.2 = ((bf16[16,2,128,128]{3,2,1,0:T(8,128)(2,1)}), bf16[16,2,128,128]{3,2,1,0:T(8,128)(2,1)S(1)}, u32[]{:S(2)}, u32[]{:S(2)}) async-start(bf16[16,2,128,128]{3,2,1,0:T(8,128)(2,1)} %copy.84), calls=%async_computation.3 | async-start | bytes 2097152 | tf_op jit(solution)/shard_map/all_to_all | solution.py:256
  209.3 84.9 %reduce-scatter.10.cloned.1.call-start = ((), (), s32[]{:S(2)}) async-start(), calls=%async_computation.10 | async-start | bytes 557056
  238.9 1.5 copy-start.11
  239.2 4.4 copy-start.9
  244.8 3.4 copy-start.4
  244.8 135.6 %reduce-scatter.6.cloned.1.call-start = ((), (), s32[]{:S(2)}) async-start(), calls=%async_computation.7 | async-start | bytes 4456448 | tf_op jit(solution)/shard_map/reduce_scatter | solution.py:218
  248.1 217.9 %reduce-scatter.8.cloned.1.call-start = ((), (), s32[]{:S(2)}) async-start(), calls=%async_computation.9 | async-start | bytes 4456448 | tf_op jit(solution)/shard_map/reduce_scatter | solution.py:279
  251.4 129.0 %copy-start.1 = (bf16[128,1024]{1,0:T(8,128)(2,1)S(1)}, bf16[128,1024]{1,0:T(8,128)(2,1)}, u32[]{:S(2)}) copy-start(bf16[128,1024]{1,0:T(8,128)(2,1)} %param.13) | copy-start | bytes 786436
  251.4 214.6 %copy-start.2 = (bf16[128,1024]{1,0:T(8,128)(2,1)S(1)}, bf16[128,1024]{1,0:T(8,128)(2,1)}, u32[]{:S(2)}) copy-start(bf16[128,1024]{1,0:T(8,128)(2,1)} %param.18) | copy-start | bytes 786436
Sparse Core Ops, SparseCore 0:
  10.4 60.3 all-gather.2
  73.3 56.2 all-gather.4
  244.9 49.2 reduce-scatter.9
  298.1 82.2 reduce-scatter.5
  383.9 82.0 reduce-scatter.7
where the time goes:
time: 476 us; the launch traced here: 474 us
  waiting for transfers between devices  322 us (68%)
  matrix products  66.3 us (14%)
  local copies, waits for them, and re-layouts  28 us (6%)
  starting transfers between devices  25.6 us (5%)
  other arithmetic  16.8 us (4%)
  between operations  14.9 us (3%)
    reduce_scatter x1, waiting for transfers between devices, local(): lax.psum_scatter(contract_cols(grad_joined, w_joined).astype(jnp.bfloat16...  83.9 us
    reduce_scatter x1, waiting for transfers between devices, local(): lax.psum_scatter(jnp.dot(outputs, w_output, preferred_element_type=jnp.fl...  82.6 us
    unnamed x6, waiting for transfers between devices  44.2 us
    all_gather x1, waiting for transfers between devices, local(): part_cot = lax.all_gather(cotangent, 'head', axis=0, tiled=True)  43 us
    all_gather x1, waiting for transfers between devices, local(): part_rows = lax.all_gather(features, 'head', axis=0, tiled=True)  41.5 us
    all_to_all x1, waiting for transfers between devices, local(): lax.all_to_all(sending.astype(jnp.bfloat16), 'dom', split_axis=0, concat_...  22.8 us
    all_to_all x1, starting transfers between devices, local(): lax.all_to_all(request, 'dom', split_axis=0, concat_axis=0, tiled=True)  9.98 us
  transfers between devices with their start and end apart: 8, of which 7 were waited for; matrix products, arithmetic and copies ran while one was open for 7% of the time, Pallas kernels for 0%

commit v1 on v0

v1 whole, which is shorter than its diff:
```python
import functools
import math

import jax
import jax.numpy as jnp
from jax import lax
from jax.experimental import pallas as pl
from jax.experimental.pallas import tpu as pltpu
from jax.sharding import PartitionSpec as P

HD = 64
BLK = 128
CAP = 2
X = 4
Y = 4
Z = 8
PARTS = 16
NBLK = 16
WIDTH = 1024
GROUP = 256
CHUNK = 512
NEG_FILL = -1e30
MESH = pl.DeviceIdType.MESH
BF = jnp.bfloat16
F32 = jnp.float32


def mm(a, b):
    return jnp.dot(a, b, preferred_element_type=F32)


def mm_nt(a, b):
    return lax.dot_general(a, b, (((1,), (1,)), ((), ())), preferred_element_type=F32)


def place():
    d = lax.axis_index("dom")
    h = lax.axis_index("head")
    return d, lax.div(h, Y), lax.rem(h, Y)


def greet(peers):
    barrier = pltpu.get_barrier_semaphore()
    for peer in peers:
        pl.semaphore_signal(barrier, inc=1, device_id=peer, device_id_type=MESH)
    pl.semaphore_wait(barrier, len(peers))


def lanes(shape):
    return lax.broadcasted_iota(jnp.int32, shape, len(shape) - 1)


def gather_kernel(
    feat, cot, w, req, qkvg, feat_t, cot_t, w_all, asked, feat_all, cot_all, stage,
    xs, xr, ys, yr, ds, dr, as_, ar,
):
    d, x, y = place()

    def dev(dd, xx, yy):
        return (dd, xx * Y + yy)

    xp, xm = lax.rem(x + 1, X), lax.rem(x + 3, X)
    yp, ym = lax.rem(y + 1, Y), lax.rem(y + 3, Y)
    x2, y2 = lax.rem(x + 2, X), lax.rem(y + 2, Y)
    right, left = dev(d, xp, y), dev(d, xm, y)
    up, down = dev(d, x, yp), dev(d, x, ym)
    across = dev(d, x, y2)
    doms = [lax.rem(d + k, PARTS) for k in range(1, PARTS)]
    greet([right, left, up, down, across] + [dev(q, x, y) for q in doms])

    def send(src, dst, s, r, to):
        c = pltpu.make_async_remote_copy(
            src_ref=src, dst_ref=dst, send_sem=s, recv_sem=r, device_id=to, device_id_type=MESH
        )
        c.start()
        return c

    pend = []
    for k, q in enumerate(doms):
        pend.append(send(req.at[q], asked.at[d], ds.at[k], dr.at[k], dev(q, x, y)))
    tables = list(pend)
    first = []
    for i, (own, full) in enumerate(((feat, feat_all), (cot, cot_all))):
        first.append(
            (
                send(own, full.at[x], xs.at[4 * i], xr.at[4 * i], right),
                send(own, full.at[x], xs.at[4 * i + 1], xr.at[4 * i + 1], left),
            )
        )
    wfirst = (
        send(w, w_all.at[y], ys.at[0], yr.at[0], up),
        send(w, w_all.at[y], ys.at[1], yr.at[1], down),
    )
    asked[d] = jnp.zeros((8, 128), jnp.int32)
    feat_all[x] = feat[...]
    cot_all[x] = cot[...]
    w_all[y] = w[...]
    rows, half = BLK // 2, WIDTH // 2
    second = []
    for i, full in enumerate((feat_all, cot_all)):
        a, b = first[i]
        a.wait_recv()
        second.append(
            send(
                full.at[xm, pl.ds(0, rows)], full.at[xm, pl.ds(0, rows)],
                xs.at[4 * i + 2], xr.at[4 * i + 2], right,
            )
        )
        b.wait_recv()
        second.append(
            send(
                full.at[xp, pl.ds(rows, rows)], full.at[xp, pl.ds(rows, rows)],
                xs.at[4 * i + 3], xr.at[4 * i + 3], left,
            )
        )
        pend += [a, b]
    wfirst[0].wait_recv()
    second.append(
        send(w_all.at[ym, pl.ds(0, half)], w_all.at[ym, pl.ds(0, half)], ys.at[2], yr.at[2], up)
    )
    wfirst[1].wait_recv()
    second.append(
        send(
            w_all.at[yp, pl.ds(half, half)], w_all.at[yp, pl.ds(half, half)],
            ys.at[3], yr.at[3], down,
        )
    )
    pend += list(wfirst)
    for c in second:
        c.wait_recv()
    pend += second
    fa = feat_all[...].reshape(X * BLK, WIDTH)
    ca = cot_all[...].reshape(X * BLK, WIDTH)
    picked = lanes((X * BLK, 256)) < 192

    def project(h):
        return jnp.where(picked, mm(fa, w_all[h]), mm(ca, w_all[h])).astype(BF).reshape(X, BLK, 256)

    back = []
    for k, (yy, to) in enumerate(((y2, across), (yp, up), (ym, down))):
        stage[k] = project(yy)
        back.append(send(stage.at[k], qkvg.at[y], as_.at[k], ar.at[k], to))
    qkvg[y] = project(y)
    for i in range(X):
        cols = pl.ds(i * BLK, BLK)
        feat_t[:, cols] = jnp.transpose(feat_all[i])
        cot_t[:, cols] = jnp.transpose(cot_all[i])
    for c in back + tables:
        c.wait_recv()
    pend += back
    for c in pend:
        c.wait_send()


def attention_kernel(
    asked, tab, qkvg, gqa, dkv, returned,
    outgoing, incoming, sending, probs, scores, kvt, qd, accq, outl, att, mrow, lrow, rl_s, rd_s,
    egrad, ks, kr, gs, gr,
):
    d, x, y = place()
    doms = [lax.rem(d + k, PARTS) for k in range(1, PARTS)]
    head = x * Y + y
    greet([(q, head) for q in doms])

    def send(src, dst, s, r, to):
        c = pltpu.make_async_remote_copy(
            src_ref=src, dst_ref=dst, send_sem=s, recv_sem=r, device_id=to, device_id_type=MESH
        )
        c.start()
        return c

    going = []
    for k, q in enumerate(doms):
        for c in range(CAP):
            outgoing[k, c] = qkvg[asked[q * CAP + c], :, :128]
        going.append(
            send(outgoing.at[k], incoming.at[pl.ds(d * CAP, CAP)], ks.at[k], kr.at[k], (q, head))
        )
    incoming[pl.ds(d * CAP, CAP)] = jnp.zeros((CAP, BLK, 128), BF)
    returned[pl.ds(d * CAP, CAP)] = jnp.zeros((CAP, BLK, 128), BF)
    low1 = lanes((BLK, 128)) < HD
    low2 = lanes((GROUP, 128)) < HD
    for s in range(NBLK):
        c, i = s // 4, s % 4
        kvt[c, :, pl.ds(i * 128, 128)] = jnp.transpose(qkvg[s, :, :128])
        part = qkvg[s, :, 128:]
        qd[s] = jnp.where(low1, part * 0.125, part)
    dkv[...] = jnp.zeros_like(dkv)

    nchunk = NBLK * BLK // CHUNK

    def fold(v, op):
        out = v[:, 0:128]
        for j in range(1, CHUNK // 128):
            out = op(out, v[:, j * 128 : (j + 1) * 128])
        return out

    def forward(g, _):
        part = qd[pl.ds(2 * g, 2)].reshape(GROUP, 128)
        qs = jnp.where(low2, part, jnp.zeros_like(part))
        top = None
        for c in range(nchunk):
            s = mm(qs, kvt[c])
            scores[c] = s
            t = fold(s, jnp.maximum)
            top = t if top is None else jnp.maximum(top, t)
        m = jnp.max(top, 1, keepdims=True)
        total, out = None, None
        for c in range(nchunk):
            e = jnp.exp(scores[c] - m)
            t = fold(e, jnp.add)
            total = t if total is None else total + t
            eb = e.astype(BF)
            probs[g, c] = eb
            o = mm(eb, qkvg[4 * c : 4 * c + 4, :, :128].reshape(CHUNK, 128))
            out = o if out is None else out + o
        l = jnp.sum(total, 1, keepdims=True)
        outl[pl.ds(2 * g, 2)] = out.reshape(2, BLK, 128)
        mrow[pl.ds(2 * g, 2)] = jnp.broadcast_to(m, (GROUP, 128)).reshape(2, BLK, 128)
        lrow[pl.ds(2 * g, 2)] = jnp.broadcast_to(l, (GROUP, 128)).reshape(2, BLK, 128)
        return 0

    lax.fori_loop(0, NBLK // 2, forward, 0)
    for c in going:
        c.wait_recv()

    def extra(s, _):
        blk = qd[s]
        zero = jnp.zeros_like(blk)
        ekv = incoming[tab[s]]
        se = mm_nt(jnp.where(low1, blk, zero), ekv)
        se = jnp.where(tab[NBLK + s] > 0, se, NEG_FILL)
        ml, ll = mrow[s], lrow[s]
        big = jnp.maximum(ml, jnp.max(se, 1, keepdims=True))
        c = jnp.exp(ml - big)
        ee = jnp.exp(se - big)
        l = c * ll + jnp.sum(ee, 1, keepdims=True)
        r = 1.0 / l
        pe = ee * r
        peb = pe.astype(BF)
        rl = c * r
        a = (outl[s] * rl + mm(peb, ekv)).astype(BF)
        go = jnp.where(low1, zero, blk)
        delta = jnp.sum(go.astype(F32) * a.astype(F32), 1, keepdims=True)
        dse = (pe * (mm_nt(go, ekv) - delta)).astype(BF)
        accq[s] = mm(dse, ekv)
        att[s] = a
        rl_s[s] = rl
        rd_s[s] = rl * delta
        bt = jnp.transpose(blk)
        egrad[s, 0:HD] = mm(bt[0:HD], dse).astype(BF)
        egrad[s, HD:128] = mm(bt[HD:128], peb).astype(BF)
        return 0

    lax.fori_loop(0, NBLK, extra, 0)
    home = []
    for k, q in enumerate(doms):
        for c in range(CAP):
            slot = q * CAP + c
            got = egrad[tab[2 * NBLK + slot]]
            sending[k, c] = jnp.where(
                tab[2 * NBLK + PARTS * CAP + slot] > 0, got, jnp.zeros_like(got)
            )
        home.append(
            send(sending.at[k], returned.at[pl.ds(d * CAP, CAP)], gs.at[k], gr.at[k], (q, head))
        )

    def backward(g, _):
        part = qd[pl.ds(2 * g, 2)].reshape(GROUP, 128)
        rl = rl_s[pl.ds(2 * g, 2)].reshape(GROUP, 128)
        rd = rd_s[pl.ds(2 * g, 2)].reshape(GROUP, 128)[:, :1]
        z = jnp.where(low2, part, (part.astype(F32) * rl).astype(BF))
        zt = jnp.transpose(z)
        go = jnp.where(low2, jnp.zeros_like(z), z)
        dq = accq[pl.ds(2 * g, 2)].reshape(GROUP, 128)
        for c in range(nchunk):
            dp = mm(go, kvt[c])
            eb = probs[g, c]
            dsc = eb * (dp - rd).astype(BF)
            dq = dq + mm(dsc, qkvg[4 * c : 4 * c + 4, :, :128].reshape(CHUNK, 128))
            dk = mm(zt[0:HD], dsc)
            dv = mm(zt[HD:128], eb)
            for i in range(CHUNK // 128):
                dkv[4 * c + i, 0:HD] += dk[:, i * 128 : (i + 1) * 128]
                dkv[4 * c + i, HD:128] += dv[:, i * 128 : (i + 1) * 128]
        both = jnp.where(low2, (dq * 0.125).astype(BF), att[pl.ds(2 * g, 2)].reshape(GROUP, 128))
        gqa[pl.ds(2 * g, 2)] = both.reshape(2, BLK, 128)
        return 0

    lax.fori_loop(0, NBLK // 2, backward, 0)
    for c in home:
        c.wait_recv()
    for c in going + home:
        c.wait_send()


def scatter_kernel(asked, dkv, returned, gkv, acc):
    acc[...] = dkv[...]

    def add(r, _):
        acc[asked[r]] += returned[r].astype(F32)
        return 0

    lax.fori_loop(0, PARTS * CAP, add, 0)

    def turn(s, _):
        gkv[s] = jnp.transpose(acc[s]).astype(BF)
        return 0

    lax.fori_loop(0, NBLK, turn, 0)


def reduce_kernel(
    gkv, gqa, feat, cot, w_all, feat_t, cot_t, lo, gf, wg,
    g_kv, g_qa, own, part, rs, wgf, sibs, sibr, ysend, yrecv, zsend, zrecv,
    as_, ar, xs, xr, ss, sr, ys, yr, zs, zr,
):
    d, x, y = place()
    core = lax.rem(d, 2)
    z = lax.div(d, 2)

    def dev(dd, xx, yy):
        return (dd, xx * Y + yy)

    ysteps = [lax.rem(y + k, Y) for k in (2, 1, 3)]
    xsteps = [lax.rem(x + k, X) for k in (2, 1, 3)]
    zsteps = [lax.rem(z + k, Z) for k in (4, 3, 5, 2, 6, 1, 7)]
    sibling = dev(d + 1 - 2 * core, x, y)
    greet(
        [dev(d, x, yy) for yy in ysteps]
        + [dev(d, xx, y) for xx in xsteps]
        + [dev(zz * 2 + core, x, y) for zz in zsteps]
        + [sibling]
    )

    def send(src, dst, s, r, to):
        c = pltpu.make_async_remote_copy(
            src_ref=src, dst_ref=dst, send_sem=s, recv_sem=r, device_id=to, device_id_type=MESH
        )
        c.start()
        return c

    a2a = []
    for k, yy in enumerate(ysteps):
        a2a.append(send(gkv.at[yy], g_kv.at[y], as_.at[2 * k], ar.at[2 * k], dev(d, x, yy)))
        a2a.append(
            send(gqa.at[yy], g_qa.at[y], as_.at[2 * k + 1], ar.at[2 * k + 1], dev(d, x, yy))
        )
    g_kv[y] = gkv[y]
    g_qa[y] = gqa[y]
    for c in a2a:
        c.wait_recv()
    rows = X * BLK
    picked = lanes((rows, 256)) < 192
    for n in range(4):
        f, o = None, None
        for h in range(Y):
            g = jnp.concatenate([g_kv[h].reshape(rows, 128), g_qa[h].reshape(rows, 128)], 1)
            wn = w_all[h, n * 256 : (n + 1) * 256, :]
            zero = jnp.zeros_like(g)
            f1 = mm_nt(jnp.where(picked, g, zero), wn)
            o1 = mm_nt(jnp.where(picked, zero, g), wn)
            f, o = (f1, o1) if f is None else (f + f1, o + o1)
        cols = pl.ds(n * 256, 256)
        part[:, 0, :, cols] = o.astype(BF).reshape(X, BLK, 256)
        part[:, 1, :, cols] = f.astype(BF).reshape(X, BLK, 256)
    rsum = []
    for k, xx in enumerate(xsteps):
        rsum.append(send(part.at[xx], rs.at[k], xs.at[k], xr.at[k], dev(d, xx, y)))
    picked_w = lanes((WIDTH, 256)) < 192
    sib = []
    for h in range(Y):
        g = jnp.concatenate([g_kv[h].reshape(rows, 128), g_qa[h].reshape(rows, 128)], 1)
        full = jnp.where(picked_w, mm(feat_t[...], g), mm(cot_t[...], g)).reshape(Z, 2, 64, 256)
        wgf[h] = full
        sibs[h] = wgf[h, :, 1 - core].astype(BF)
        sib.append(send(sibs.at[h], sibr.at[h], ss.at[h], sr.at[h], sibling))
    for c in sib:
        c.wait_recv()
    ysum = []
    for k, yy in enumerate(ysteps):
        ysend[k] = (wgf[yy, :, core] + sibr[yy].astype(F32)).astype(BF)
        ysum.append(send(ysend.at[k], yrecv.at[k], ys.at[k], yr.at[k], dev(d, x, yy)))
    total = wgf[y, :, core] + sibr[y].astype(F32)
    for c in rsum:
        c.wait_recv()
    base = part[x].astype(F32)
    for k in range(3):
        base = base + rs[k].astype(F32)
    lo[...] = (feat[...].astype(F32) + base[0]).astype(BF)
    gf[...] = (cot[...].astype(F32) + base[1]).astype(BF)
    for k in range(3):
        ysum[k].wait_recv()
        total = total + yrecv[k].astype(F32)
    zsend[...] = total.astype(BF)
    own[...] = total
    zsum = []
    for k, zz in enumerate(zsteps):
        zsum.append(
            send(zsend.at[zz], zrecv.at[k], zs.at[k], zr.at[k], dev(zz * 2 + core, x, y))
        )
    res = own[z]
    for k in range(7):
        zsum[k].wait_recv()
        res = res + zrecv[k].astype(F32)
    wg[...] = res
    for c in a2a + rsum + sib + ysum + zsum:
        c.wait_send()


VM = pl.BlockSpec(memory_space=pltpu.VMEM)
SM = pl.BlockSpec(memory_space=pltpu.SMEM)


def dma(n):
    return pltpu.SemaphoreType.DMA((n,))


def sds(shape, dtype):
    return jax.ShapeDtypeStruct(shape, dtype)


def params(cid):
    return pltpu.CompilerParams(
        collective_id=cid, has_side_effects=True, vmem_limit_bytes=56 * 1024 * 1024
    )


def turned(t):
    return (t % 4) * 4 + t // 4


def local(
    features, w_query, w_key, w_value, w_output, cotangent, cross_source, cross_target, cross_count
):
    source, target, live_count = cross_source[0], cross_target[0], cross_count[0]
    owners = source // NBLK
    slot_ids = jnp.arange(16, dtype=jnp.int32)
    earlier = (owners[:, None] == owners[None, :]) & (slot_ids[None, :] < slot_ids[:, None])
    position = jnp.sum(earlier.astype(jnp.int32), 1)
    slot = owners * CAP + position
    placed = slot[:, None] == jnp.arange(PARTS * CAP, dtype=jnp.int32)[None, :]
    live = slot_ids < live_count
    request = jnp.sum(jnp.where(placed, turned(source % NBLK)[:, None], 0), 0)
    req = jnp.pad(request.reshape(PARTS, 1, CAP), ((0, 0), (0, 7), (0, 126)))
    tpos = turned(target)
    chosen = (tpos[:, None] == slot_ids[None, :]) & live[:, None]
    alive = placed & live[:, None]
    tab = jnp.concatenate(
        [
            jnp.sum(jnp.where(chosen, slot[:, None], 0), 0),
            jnp.sum(chosen.astype(jnp.int32), 0),
            jnp.sum(jnp.where(alive, tpos[:, None], 0), 0),
            jnp.sum(alive.astype(jnp.int32), 0),
        ]
    )
    w = jnp.concatenate([w_key, w_value, w_query, w_output.T], 1)

    qkvg, feat_t, cot_t, w_all, asked = pl.pallas_call(
        gather_kernel,
        out_shape=(
            sds((Y, X, BLK, 256), BF),
            sds((WIDTH, X * BLK), BF),
            sds((WIDTH, X * BLK), BF),
            sds((Y, WIDTH, 256), BF),
            sds((PARTS, 8, 128), jnp.int32),
        ),
        in_specs=[VM] * 4,
        out_specs=(VM,) * 5,
        scratch_shapes=[
            pltpu.VMEM((X, BLK, WIDTH), BF),
            pltpu.VMEM((X, BLK, WIDTH), BF),
            pltpu.VMEM((3, X, BLK, 256), BF),
            dma(8), dma(8), dma(4), dma(4), dma(15), dma(15), dma(3), dma(3),
        ],
        compiler_params=params(1),
        name="gather_project",
    )(features, cotangent, w, req)
    asked = asked[:, 0, :CAP].reshape(PARTS * CAP)

    gqa, dkv, returned = pl.pallas_call(
        attention_kernel,
        out_shape=(
            sds((NBLK, BLK, 128), BF),
            sds((NBLK, 128, BLK), F32),
            sds((PARTS * CAP, 128, BLK), BF),
        ),
        in_specs=[SM, SM, VM],
        out_specs=(VM,) * 3,
        scratch_shapes=[
            pltpu.VMEM((15, CAP, BLK, 128), BF),
            pltpu.VMEM((PARTS * CAP, BLK, 128), BF),
            pltpu.VMEM((15, CAP, 128, BLK), BF),
            pltpu.VMEM((NBLK // 2, 4, GROUP, CHUNK), BF),
            pltpu.VMEM((4, GROUP, CHUNK), F32),
            pltpu.VMEM((4, 128, CHUNK), BF),
            pltpu.VMEM((NBLK, BLK, 128), BF),
            pltpu.VMEM((NBLK, BLK, 128), F32),
            pltpu.VMEM((NBLK, BLK, 128), F32),
            pltpu.VMEM((NBLK, BLK, 128), BF),
            pltpu.VMEM((NBLK, BLK, 128), F32),
            pltpu.VMEM((NBLK, BLK, 128), F32),
            pltpu.VMEM((NBLK, BLK, 128), F32),
            pltpu.VMEM((NBLK, BLK, 128), F32),
            pltpu.VMEM((NBLK, 128, BLK), BF),
            dma(15), dma(15), dma(15), dma(15),
        ],
        compiler_params=params(2),
        name="attention",
    )(asked, tab, qkvg.reshape(NBLK, BLK, 256))

    gkv = pl.pallas_call(
        scatter_kernel,
        out_shape=sds((NBLK, BLK, 128), BF),
        in_specs=[SM, VM, VM],
        out_specs=VM,
        scratch_shapes=[pltpu.VMEM((NBLK, 128, BLK), F32)],
        name="scatter_add",
    )(asked, dkv, returned)

    four = (Y, X, BLK, 128)
    layer_out, grad_features, wg = pl.pallas_call(
        reduce_kernel,
        out_shape=(
            sds((BLK, WIDTH), BF),
            sds((BLK, WIDTH), BF),
            sds((64, 256), F32),
        ),
        in_specs=[VM] * 7,
        out_specs=(VM,) * 3,
        scratch_shapes=[
            pltpu.VMEM(four, BF),
            pltpu.VMEM(four, BF),
            pltpu.VMEM((Z, 64, 256), F32),
            pltpu.VMEM((X, 2, BLK, WIDTH), BF),
            pltpu.VMEM((3, 2, BLK, WIDTH), BF),
            pltpu.VMEM((Y, Z, 2, 64, 256), F32),
            pltpu.VMEM((Y, Z, 64, 256), BF),
            pltpu.VMEM((Y, Z, 64, 256), BF),
            pltpu.VMEM((3, Z, 64, 256), BF),
            pltpu.VMEM((3, Z, 64, 256), BF),
            pltpu.VMEM((Z, 64, 256), BF),
            pltpu.VMEM((7, 64, 256), BF),
            dma(6), dma(6), dma(3), dma(3), dma(4), dma(4), dma(3), dma(3), dma(7), dma(7),
        ],
        compiler_params=params(3),
        name="project_reduce",
    )(gkv.reshape(four), gqa.reshape(four), features, cotangent, w_all, feat_t, cot_t)
    return (
        layer_out,
        grad_features,
        wg[:, 128:192],
        wg[:, 0:64],
        wg[:, 64:128],
        wg[:, 192:256],
    )


def solution(mesh):
    return jax.shard_map(
        local,
        mesh=mesh,
        in_specs=(
            P(("dom", "head"), None),
            P(None, "head"),
            P(None, "head"),
            P(None, "head"),
            P("head", None),
            P(("dom", "head"), None),
            P("dom", None),
            P("dom", None),
            P("dom"),
        ),
        out_specs=(
            P(("dom", "head"), None),
            P(("dom", "head"), None),
            P("dom", "head"),
            P("dom", "head"),
            P("dom", "head"),
            P("dom", "head"),
        ),
        check_vma=False,
    )
```

time: 476 us -> 194 us (0.41)
  waiting for transfers between devices: 322 us -> 0 us
  Pallas kernels: 0 us -> 177 us
  matrix products: 66.3 us -> 0 us
  starting transfers between devices: 25.6 us -> 0 us
  local copies, waits for them, and re-layouts: 28 us -> 11.4 us
  between operations: 14.9 us -> 1.35 us
  other arithmetic: 16.8 us -> 3.49 us
    pallas_call x0 -> x4, Pallas kernels: none -> 177 us  [the longest x1 65.7 us: local(): pl.pallas_call(attention_kernel, out_shape=(sds((NBLK, BLK, 128), BF), sd...]
    reduce_scatter x2 -> x0, waiting for transfers between devices: 166 us -> none  [the longest x1 83.9 us: local(): lax.psum_scatter(contract_cols(grad_joined, w_joined).astype(jnp.bfloat16...]
    all_gather x2 -> x0, waiting for transfers between devices: 84.5 us -> none  [the longest x1 43 us: local(): part_cot = lax.all_gather(cotangent, 'head', axis=0, tiled=True)]
    dot_general x66 -> x0, matrix products: 66.3 us -> none  [the longest x2 6.86 us: contract_rows(): lax.dot_general(left, right, (((0,), (0,)), ((), ())), preferred_element_...]
    unnamed x6 -> x0, waiting for transfers between devices: 44.2 us -> none
    all_to_all x3 -> x0, waiting for transfers between devices: 27 us -> none  [the longest x1 22.8 us: local(): lax.all_to_all(sending.astype(jnp.bfloat16), 'dom', split_axis=0, concat_...]
    all_to_all x3 -> x0, starting transfers between devices: 25.4 us -> none  [the longest x1 9.98 us: local(): lax.all_to_all(request, 'dom', split_axis=0, concat_axis=0, tiled=True)]
    reduce_sum x21 -> x2, other arithmetic: 7.29 us -> 0.19 us  [the longest x1 0.1 us: local(): jnp.sum(jnp.where(alive, tpos[:, None], 0), 0)]
  transfers between devices with their start and end apart: 8 -> 0, of which waited for: 7 -> 0; matrix products, arithmetic and copies ran while one was open for 7% -> 0% of each run, Pallas kernels for 0% -> 0%
where the time goes in v1:
time: 194 us; the launch traced here: 193 us
  Pallas kernels  177 us (91%)
  local copies, waits for them, and re-layouts  11.4 us (6%)
  other arithmetic  3.49 us (2%)
    pallas_call x1, Pallas kernels, local(): pl.pallas_call(attention_kernel, out_shape=(sds((NBLK, BLK, 128), BF), sd...  65.7 us
    pallas_call x1, Pallas kernels, local(): pl.pallas_call(reduce_kernel, out_shape=(sds((BLK, WIDTH), BF), sds((BLK,...  57.8 us
    pallas_call x1, Pallas kernels, local(): pl.pallas_call(gather_kernel, out_shape=(sds((Y, X, BLK, 256), BF), sds((...  49.3 us
    unnamed x6, local copies, waits for them, and re-layouts  7.64 us
    pallas_call x1, Pallas kernels, local(): pl.pallas_call(scatter_kernel, out_shape=sds((NBLK, BLK, 128), BF), in_sp...  4.37 us

profile of v1, /device:TPU:1, one launch (start us, length us, event | category | flops | bytes accessed | tf_op | source)
XLA Modules:
  0.0 193.3 jit_solution(14980853617658012629)
XLA Ops:
  1.3 0.7 fusion.7
  2.0 0.7 fusion.4
  2.6 0.2 convert_reduce_fusion.2
  2.8 0.1 select_reduce_fusion
  2.9 0.1 select_reduce_fusion.1
  3.0 0.6 pad_add_fusion.tab
  3.6 0.1 reshape.168
  3.7 0.6 pad.4.req
  4.3 1.1 copy.28
  5.4 1.1 copy.26
  6.5 1.1 copy.27
  7.6 1.1 copy.25
  8.7 1.2 pad_maximum_fusion.w
  9.8 49.3 %gather_project.1 = (bf16[4,4,128,256]{3,2,1,0:T(8,128)(2,1)}, bf16[1024,512]{1,0:T(8,128)(2,1)}, bf16[1024,512]{1,0:T(8,128)(2,1)}, bf16[4,1024,256]{2,1,0:T(8,128)(2,1)}, s32[16,8,128]{2,1,0:T(8,128)}) custom-call(bf16[128,1024]{1,0:T(8,128)(2,1)} %feat.3, bf16[128,1024]{1,0:T(8,128)(2,1)} %cot.3, bf16[1024,256]{1,0:T(8,128)(2,1)} %pad_maximum_fusion.w, ...), custom_call_target="tpu_custom_call" | custom-call | tf_op jit(solution)/shard_map/gather_project/pallas_call | solution.py:459
  59.1 0.9 slice_reduce_fusion
  60.0 0.6 reshape_squeeze.3.asked
  60.6 65.7 %attention.1 = (bf16[16,128,128]{2,1,0:T(8,128)(2,1)}, f32[16,128,128]{2,1,0:T(8,128)}, bf16[32,128,128]{2,1,0:T(8,128)(2,1)}) custom-call(s32[32]{0:T(128)} %reshape_squeeze.3.asked, s32[96]{0:T(128)} %pad_add_fusion.tab, bf16[16,128,256]{2,1,0:T(8,128)(2,1)} %bitcast.38), custom_call_target="tpu_custom_call" | custom-call | tf_op jit(solution)/shard_map/attention/pallas_call | solution.py:481
  126.3 4.4 %scatter_add.1 = bf16[16,128,128]{2,1,0:T(8,128)(2,1)} custom-call(s32[32]{0:T(128)} %reshape_squeeze.3.asked, f32[16,128,128]{2,1,0:T(8,128)} %get-tuple-element.19.dkv, bf16[32,128,128]{2,1,0:T(8,128)(2,1)} %get-tuple-element.20.returned), custom_call_target="tpu_custom_call" | custom-call | tf_op jit(solution)/shard_map/scatter_add/pallas_call | solution.py:512
  130.6 57.8 %project_reduce.1 = (bf16[128,1024]{1,0:T(8,128)(2,1)}, bf16[128,1024]{1,0:T(8,128)(2,1)}, f32[64,256]{1,0:T(8,128)}) custom-call(bf16[4,4,128,128]{3,2,1,0:T(8,128)(2,1)} %bitcast.37, bf16[4,4,128,128]{3,2,1,0:T(8,128)(2,1)} %bitcast.40, bf16[128,1024]{1,0:T(8,128)(2,1)} %feat.3, bf16[128,1024]{1,0:T(8,128)(2,1)} %cot.3, ...), custom_call_target="tpu_custom_call" | custom-call | tf_op jit(solution)/shard_map/project_reduce/pallas_call | solution.py:522
  188.4 1.6 fusion.8
  190.0 1.7 copy.33
  191.7 1.7 copy.34
  (2 shorter events, 0.0 us)

commit v2 on v1

v2 whole, which is shorter than its diff:
```python
import jax
import jax.numpy as jnp
from jax import lax
from jax.experimental import pallas as pl
from jax.experimental.pallas import tpu as pltpu
from jax.sharding import PartitionSpec as P

HD = 64
BLK = 128
CAP = 2
X = 4
Y = 4
Z = 8
PARTS = 16
NBLK = 16
WIDTH = 1024
GROUP = 256
CHUNK = 512
NEG_FILL = -1e30
MESH = pl.DeviceIdType.MESH
BF = jnp.bfloat16
F32 = jnp.float32


def mm(a, b):
    return jnp.dot(a, b, preferred_element_type=F32)


def mm_nt(a, b):
    return lax.dot_general(a, b, (((1,), (1,)), ((), ())), preferred_element_type=F32)


def place():
    d = lax.axis_index("dom")
    h = lax.axis_index("head")
    return d, lax.div(h, Y), lax.rem(h, Y)


def greet(peers):
    barrier = pltpu.get_barrier_semaphore()
    for peer in peers:
        pl.semaphore_signal(barrier, inc=1, device_id=peer, device_id_type=MESH)
    pl.semaphore_wait(barrier, len(peers))


def lanes(shape):
    return lax.broadcasted_iota(jnp.int32, shape, len(shape) - 1)


class Sems:
    def __init__(self, send, recv):
        self.send, self.recv, self.n, self.all = send, recv, 0, []

    def start(self, src, dst, to):
        c = pltpu.make_async_remote_copy(
            src_ref=src, dst_ref=dst, send_sem=self.send.at[self.n], recv_sem=self.recv.at[self.n],
            device_id=to, device_id_type=MESH,
        )
        c.start()
        self.n += 1
        self.all.append(c)
        return c


def order_tables(asked, table):
    sub = lax.broadcasted_iota(jnp.int32, (128, 128), 0)
    lane = lax.broadcasted_iota(jnp.int32, (128, 128), 1)
    a = jnp.where((sub & 7) < CAP, asked[...].reshape(128, 128), 99.0)
    b = jnp.transpose(a)
    one, zero = jnp.ones((128, 128), F32), jnp.zeros((128, 128), F32)
    lanef = lane.astype(F32)
    less = jnp.where((b < a) | ((b == a) & (lane < sub)), one, zero)
    rank = jnp.sum(less, 1, keepdims=True)
    hot = jnp.where(rank == lanef, one, zero)
    where_from = ((sub >> 3) * CAP + (sub & 7)).astype(F32)
    order = jnp.sum(hot * where_from, 0, keepdims=True)
    value = jnp.sum(hot * a, 0, keepdims=True)
    end = jnp.sum(jnp.where(a <= lanef, one, zero), 0, keepdims=True) - 1.0
    has = jnp.sum(jnp.where(a == lanef, one, zero), 0, keepdims=True)
    wide = jnp.broadcast_to(value, (8, 128))
    same = jnp.where(wide == pltpu.roll(wide, 1, 1), one[:8], zero[:8])
    row = sub[:8]
    out = jnp.where(row == 0, jnp.minimum(b[:8], 15.0), zero[:8])
    for i, v in ((1, order), (2, same), (3, jnp.maximum(end, 0.0)), (4, has)):
        out = jnp.where(row == i, jnp.broadcast_to(v, (8, 128)), out)
    table[...] = out.astype(jnp.int32)


def layer_kernel(
    tab, feat, cot, wk, wv, wq, wo, req,
    lo, gf, wg,
    feat_all, cot_all, wkv, wqo, feat_t, cot_t, asked, table, smem, kst, qst, kv_l, qg_l,
    outgoing, incoming, sending, returned, probs, scores, kvt, qd, accq, outl, mrow, lrow, rl_s, rd_s,
    dkv, egrad, runs, gkv, attp, gqp, g_kv, at_l, gq_l, part, rs, g2, wgf, sibs, sibr, ysend, yrecv,
    own, zsend, zrecv, send_sems, recv_sems, local_sem,
):
    d, x, y = place()
    core, z = lax.rem(d, 2), lax.div(d, 2)

    def dev(dd, xx, yy):
        return (dd, xx * Y + yy)

    xp, xm, x2 = [lax.rem(x + k, X) for k in (1, 3, 2)]
    yp, ym, y2 = [lax.rem(y + k, Y) for k in (1, 3, 2)]
    right, left, xopp = dev(d, xp, y), dev(d, xm, y), dev(d, x2, y)
    up, down, yopp = dev(d, x, yp), dev(d, x, ym), dev(d, x, y2)
    doms = [lax.rem(d + k, PARTS) for k in range(1, PARTS)]
    sibling = dev(d + 1 - 2 * core, x, y)
    greet([right, left, xopp, up, down, yopp] + [dev(q, x, y) for q in doms])
    net = Sems(send_sems, recv_sems)
    start = net.start
    ysteps = [(y2, yopp), (yp, up), (ym, down)]

    fl = start(feat, feat_all.at[x], right)
    fr = start(feat, feat_all.at[x], left)
    for i, (w, o) in enumerate(((wkv, (wk, wv)), (wqo, (wq, wo)))):
        w[y, 0:HD] = o[0][...]
        w[y, HD:128] = o[1][...]
    mine = pl.multiple_of(core * HD, HD)
    whole = pl.ds(mine, HD)
    upper, lower = pl.ds(mine, 32), pl.ds(mine + 32, 32)
    wown = []
    for w in (wkv, wqo):
        piece = w.at[y, whole]
        wown.append((start(piece, piece, up), start(piece, piece, down)))
    tables = [start(req.at[q], asked.at[d], dev(q, x, y)) for q in doms]
    asked[d] = jnp.full((8, 128), 99.0, F32)
    feat_all[x] = feat[...]
    cot_all[x] = cot[...]

    def wmiddle(i):
        w = (wkv, wqo)[i]
        a, b = wown[i]
        a.wait_recv()
        p = w.at[ym, upper]
        f1 = start(p, p, up)
        p = w.at[ym, whole]
        s1 = start(p, p, sibling)
        b.wait_recv()
        p = w.at[yp, lower]
        f2 = start(p, p, down)
        p = w.at[yp, whole]
        s2 = start(p, p, sibling)
        return f1, f2, s1, s2

    def wlast(i, mid):
        w = (wkv, wqo)[i]
        mid[0].wait_recv()
        mid[1].wait_recv()
        p = w.at[y2, whole]
        s3 = start(p, p, sibling)
        mid[2].wait_recv()
        mid[3].wait_recv()
        s3.wait_recv()

    def xmiddle(full, a, b):
        a.wait_recv()
        p = full.at[xm, pl.ds(0, HD)]
        f1 = start(p, p, right)
        b.wait_recv()
        p = full.at[xp, pl.ds(HD, HD)]
        f2 = start(p, p, left)
        return f1, f2

    mkv = wmiddle(0)
    ffwd = xmiddle(feat_all, fl, fr)
    cl = start(cot, cot_all.at[x], right)
    cr = start(cot, cot_all.at[x], left)
    mqo = wmiddle(1)
    wlast(0, mkv)
    low4 = (lanes((BLK, 512)) & 127) < HD

    def project_kv(b):
        r = mm_nt(feat_all[b], wkv[...].reshape(Y * 128, WIDTH)).astype(BF)
        for h in range(Y):
            kst[h, b] = r[:, h * 128 : (h + 1) * 128]
        kv_l[y, b] = kst[y, b]
        return [start(kst.at[yy, b], kv_l.at[y, b], to) for yy, to in ysteps]

    def project_qo(b):
        w = wqo[...].reshape(Y * 128, WIDTH)
        r = jnp.where(low4, mm_nt(feat_all[b], w), mm_nt(cot_all[b], w)).astype(BF)
        for h in range(Y):
            qst[h, b] = r[:, h * 128 : (h + 1) * 128]
        qg_l[y, b] = qst[y, b]
        return [start(qst.at[yy, b], qg_l.at[y, b], to) for yy, to in ysteps]

    def turn(full, b, out):
        out[b] = jnp.transpose(full[b])

    kvs = project_kv(x)
    kvs += project_kv(xm)
    kvs += project_kv(xp)
    for c in tables:
        c.wait_recv()
    order_tables(asked, table)
    cp = pltpu.make_async_copy(table, smem, local_sem)
    cp.start()
    for c in ffwd:
        c.wait_recv()
    kvs += project_kv(x2)
    wlast(1, mqo)
    qgs = project_qo(x)
    cfwd = xmiddle(cot_all, cl, cr)
    qgs += project_qo(xm)
    qgs += project_qo(xp)
    cp.wait()
    for c in kvs:
        c.wait_recv()

    going = []
    for k, q in enumerate(doms):
        for c in range(CAP):
            at = jnp.clip(smem[0, q * 8 + c], 0, NBLK - 1)
            outgoing[k, c] = kv_l[lax.div(at, 4), lax.rem(at, 4)]
        going.append(start(outgoing.at[k], incoming.at[pl.ds(d * CAP, CAP)], dev(q, x, y)))
    for c in cfwd:
        c.wait_recv()
    qgs += project_qo(x2)
    incoming[pl.ds(d * CAP, CAP)] = jnp.zeros((CAP, BLK, 128), BF)
    returned[pl.ds(d * CAP, CAP)] = jnp.zeros((CAP, BLK, 128), BF)
    for b in range(X):
        turn(feat_all, b, feat_t)
        turn(cot_all, b, cot_t)
    low1 = lanes((BLK, 128)) < HD
    low2 = lanes((GROUP, 128)) < HD
    for s in range(NBLK):
        kvt[s // 4, :, pl.ds((s % 4) * 128, 128)] = jnp.transpose(kv_l[s // 4, s % 4])
    for c in qgs:
        c.wait_recv()
    for s in range(NBLK):
        p = qg_l[s // 4, s % 4]
        qd[s] = jnp.where(low1, p * 0.125, p)
    dkv[...] = jnp.zeros_like(dkv)

    nchunk = NBLK * BLK // CHUNK

    def fold(v, op):
        out = v[:, 0:128]
        for j in range(1, CHUNK // 128):
            out = op(out, v[:, j * 128 : (j + 1) * 128])
        return out

    def forward(g, _):
        p = qd[pl.ds(2 * g, 2)].reshape(GROUP, 128)
        qs = jnp.where(low2, p, jnp.zeros_like(p))
        top = None
        for c in range(nchunk):
            s = mm(qs, kvt[c])
            scores[c] = s
            t = fold(s, jnp.maximum)
            top = t if top is None else jnp.maximum(top, t)
        m = jnp.max(top, 1, keepdims=True)
        total, out = None, None
        for c in range(nchunk):
            e = jnp.exp(scores[c] - m)
            t = fold(e, jnp.add)
            total = t if total is None else total + t
            eb = e.astype(BF)
            probs[g, c] = eb
            o = mm(eb, kv_l[c].reshape(CHUNK, 128))
            out = o if out is None else out + o
        l = jnp.sum(total, 1, keepdims=True)
        outl[pl.ds(2 * g, 2)] = out.reshape(2, BLK, 128)
        mrow[pl.ds(2 * g, 2)] = jnp.broadcast_to(m, (GROUP, 128)).reshape(2, BLK, 128)
        lrow[pl.ds(2 * g, 2)] = jnp.broadcast_to(l, (GROUP, 128)).reshape(2, BLK, 128)
        return 0

    lax.fori_loop(0, NBLK // 2, forward, 0)
    for c in going:
        c.wait_recv()

    def extra(s):
        blk = qd[s]
        zero = jnp.zeros_like(blk)
        ekv = incoming[tab[s]]
        se = mm_nt(jnp.where(low1, blk, zero), ekv)
        se = jnp.where(tab[NBLK + s] > 0, se, NEG_FILL)
        ml, ll = mrow[s], lrow[s]
        big = jnp.maximum(ml, jnp.max(se, 1, keepdims=True))
        c = jnp.exp(ml - big)
        ee = jnp.exp(se - big)
        l = c * ll + jnp.sum(ee, 1, keepdims=True)
        r = 1.0 / l
        pe = ee * r
        peb = pe.astype(BF)
        rl = c * r
        out = (outl[s] * rl + mm(peb, ekv)).astype(BF).astype(F32)
        go = jnp.where(low1, zero, blk)
        delta = jnp.sum(go.astype(F32) * out, 1, keepdims=True)
        dse = (pe * (mm_nt(go, ekv) - delta)).astype(BF)
        accq[s] = mm(dse, ekv)
        rl_s[s] = rl
        rd_s[s] = rl * delta
        bt = jnp.transpose(blk)
        egrad[s, 0:HD] = mm(bt[0:HD], dse).astype(BF)
        egrad[s, HD:128] = mm(bt[HD:128], peb).astype(BF)
        return out

    def extras(g, _):
        a, b = extra(2 * g), extra(2 * g + 1)
        attp[lax.div(g, 2), lax.rem(g, 2)] = jnp.where(low1, pltpu.roll(a, HD, 1), b).astype(BF)
        return 0

    lax.fori_loop(0, NBLK // 2, extras, 0)
    home = []
    for k, q in enumerate(doms):
        for c in range(CAP):
            slot = q * CAP + c
            got = egrad[tab[2 * NBLK + slot]]
            sending[k, c] = jnp.where(
                tab[2 * NBLK + PARTS * CAP + slot] > 0, got, jnp.zeros_like(got)
            )
        home.append(start(sending.at[k], returned.at[pl.ds(d * CAP, CAP)], dev(q, x, y)))
    ats = [start(attp.at[yy], at_l.at[y], to) for yy, to in ysteps]
    at_l[y] = attp[y]

    def backward(g, _):
        p = qd[pl.ds(2 * g, 2)].reshape(GROUP, 128)
        rl = rl_s[pl.ds(2 * g, 2)].reshape(GROUP, 128)
        rd = rd_s[pl.ds(2 * g, 2)].reshape(GROUP, 128)[:, :1]
        zz = jnp.where(low2, p, (p.astype(F32) * rl).astype(BF))
        zt = jnp.transpose(zz)
        go = jnp.where(low2, jnp.zeros_like(zz), zz)
        dq = accq[pl.ds(2 * g, 2)].reshape(GROUP, 128)
        for c in range(nchunk):
            dp = mm(go, kvt[c])
            eb = probs[g, c]
            dsc = eb * (dp - rd).astype(BF)
            dq = dq + mm(dsc, kv_l[c].reshape(CHUNK, 128))
            dk = mm(zt[0:HD], dsc)
            dv = mm(zt[HD:128], eb)
            for i in range(CHUNK // 128):
                dkv[4 * c + i, 0:HD] += dk[:, i * 128 : (i + 1) * 128]
                dkv[4 * c + i, HD:128] += dv[:, i * 128 : (i + 1) * 128]
        dq = dq * 0.125
        gqp[lax.div(g, 2), lax.rem(g, 2)] = jnp.where(
            low1, dq[0:BLK], pltpu.roll(dq[BLK:GROUP], HD, 1)
        ).astype(BF)
        return 0

    lax.fori_loop(0, NBLK // 2, backward, 0)
    gqs = [start(gqp.at[yy], gq_l.at[y], to) for yy, to in ysteps]
    gq_l[y] = gqp[y]

    rows = X * BLK
    for c in ats:
        c.wait_recv()
    for h in range(Y):
        for j in range(2):
            p = at_l[h, j].astype(F32)
            zero = jnp.zeros_like(p)
            g2[1, h, 2 * j] = jnp.where(low1, zero, pltpu.roll(p, HD, 1)).astype(BF)
            g2[1, h, 2 * j + 1] = jnp.where(low1, zero, p).astype(BF)
    for n in range(4):
        cols = pl.ds(n * 256, 256)
        o = None
        for h in range(Y):
            t = mm(g2[1, h].reshape(rows, 128), wqo[h, :, cols])
            o = t if o is None else o + t
        part[:, 0, :, cols] = o.astype(BF).reshape(X, BLK, 256)
    xsteps = [(x2, xopp), (xp, right), (xm, left)]
    los = [start(part.at[xx, 0], rs.at[k, 0], to) for k, (xx, to) in enumerate(xsteps)]

    def tmm(t, g):
        r = None
        for b in range(X):
            v = mm(t[b], g[b])
            r = v if r is None else r + v
        return r

    def weights(i, left_of):
        out = []
        for h in range(Y):
            wgf[i, h] = left_of(h).reshape(Z, 2, 64, 128)
            sibs[i, h] = wgf[i, h, :, 1 - core].astype(BF)
            out.append(start(sibs.at[i, h], sibr.at[i, h], sibling))
        return out

    def along_y(i, sib):
        for c in sib:
            c.wait_recv()
        out = []
        for k, (yy, to) in enumerate(ysteps):
            ysend[i, k] = (wgf[i, yy, :, core] + sibr[i, yy].astype(F32)).astype(BF)
            out.append(start(ysend.at[i, k], yrecv.at[i, k], to))
        return out

    zsteps = [lax.rem(z + k, Z) for k in (4, 3, 5, 2, 6, 1, 7)]

    def along_z(i, ys):
        total = wgf[i, y, :, core] + sibr[i, y].astype(F32)
        for k in range(3):
            ys[k].wait_recv()
            total = total + yrecv[i, k].astype(F32)
        own[i] = total
        zsend[i] = total.astype(BF)
        return [
            start(zsend.at[i, zz], zrecv.at[i, k], dev(zz * 2 + core, x, y))
            for k, zz in enumerate(zsteps)
        ]

    def finish(i, zsum):
        res = own[i, z]
        for k in range(7):
            zsum[k].wait_recv()
            res = res + zrecv[i, k].astype(F32)
        wg[:, i * 128 : (i + 1) * 128] = res

    for c in gqs:
        c.wait_recv()
    for h in range(Y):
        for j in range(2):
            p = gq_l[h, j].astype(F32)
            zero = jnp.zeros_like(p)
            g2[0, h, 2 * j] = jnp.where(low1, p, zero).astype(BF)
            g2[0, h, 2 * j + 1] = jnp.where(low1, pltpu.roll(p, HD, 1), zero).astype(BF)
    sib1 = weights(1, lambda h: tmm(feat_t, g2[0, h]) + tmm(cot_t, g2[1, h]))
    y1 = along_y(1, sib1)
    for c in home:
        c.wait_recv()
    running = None
    for k in range(CAP * (PARTS - 1)):
        got = returned[jnp.clip(smem[1, k], 0, PARTS * CAP - 1)].astype(F32)
        running = got if k == 0 else got + running * smem[2, k].astype(F32)
        runs[k] = running
    for s in range(NBLK):
        more = jnp.where(smem[4, s] > 0, runs[jnp.clip(smem[3, s], 0, CAP * (PARTS - 1) - 1)], jnp.zeros((128, BLK), F32))
        gkv[s // 4, s % 4] = jnp.transpose(dkv[s] + more).astype(BF)
    gks = [start(gkv.at[yy], g_kv.at[y], to) for yy, to in ysteps]
    g_kv[y] = gkv[y]
    z1 = along_z(1, y1)
    for c in gks:
        c.wait_recv()
    for n in range(4):
        cols = pl.ds(n * 256, 256)
        o = None
        for h in range(Y):
            t = mm(g2[0, h].reshape(rows, 128), wqo[h, :, cols])
            t = t + mm(g_kv[h].reshape(rows, 128), wkv[h, :, cols])
            o = t if o is None else o + t
        part[:, 1, :, cols] = o.astype(BF).reshape(X, BLK, 256)
    gfs = [start(part.at[xx, 1], rs.at[k, 1], to) for k, (xx, to) in enumerate(xsteps)]
    sib0 = weights(0, lambda h: tmm(feat_t, g_kv[h]))
    y0 = along_y(0, sib0)
    for i, (copies, base, out) in enumerate(((los, feat, lo), (gfs, cot, gf))):
        if i == 1:
            finish(1, z1)
            z0 = along_z(0, y0)
        total = part[x, i].astype(F32)
        for k in range(3):
            copies[k].wait_recv()
            total = total + rs[k, i].astype(F32)
        out[...] = (base[...].astype(F32) + total).astype(BF)
    finish(0, z0)
    for c in net.all:
        c.wait_send()


VM = pl.BlockSpec(memory_space=pltpu.VMEM)
SM = pl.BlockSpec(memory_space=pltpu.SMEM)
COPIES = 134


def sds(shape, dtype):
    return jax.ShapeDtypeStruct(shape, dtype)


def params(cid):
    return pltpu.CompilerParams(
        collective_id=cid, has_side_effects=True, vmem_limit_bytes=60 * 1024 * 1024
    )


def turned(t):
    return (t % 4) * 4 + t // 4


def local(
    features, w_query, w_key, w_value, w_output, cotangent, cross_source, cross_target, cross_count
):
    source, target, live_count = cross_source[0], cross_target[0], cross_count[0]
    owners = source // NBLK
    slot_ids = jnp.arange(16, dtype=jnp.int32)
    earlier = (owners[:, None] == owners[None, :]) & (slot_ids[None, :] < slot_ids[:, None])
    position = jnp.sum(earlier.astype(jnp.int32), 1)
    slot = owners * CAP + position
    placed = slot[:, None] == jnp.arange(PARTS * CAP, dtype=jnp.int32)[None, :]
    live = slot_ids < live_count
    row_slot = jnp.arange(PARTS * 8, dtype=jnp.int32)
    row_slot = jnp.where(row_slot % 8 < CAP, (row_slot // 8) * CAP + row_slot % 8, -1)
    placed_row = slot[:, None] == row_slot[None, :]
    request = jnp.sum(jnp.where(placed_row, turned(source % NBLK)[:, None], 0), 0)
    req = jnp.broadcast_to(request.astype(F32).reshape(PARTS, 8, 1), (PARTS, 8, 128))
    tpos = turned(target)
    chosen = (tpos[:, None] == slot_ids[None, :]) & live[:, None]
    alive = placed & live[:, None]
    tab = jnp.concatenate(
        [
            jnp.sum(jnp.where(chosen, slot[:, None], 0), 0),
            jnp.sum(chosen.astype(jnp.int32), 0),
            jnp.sum(jnp.where(alive, tpos[:, None], 0), 0),
            jnp.sum(alive.astype(jnp.int32), 0),
        ]
    )
    v = pltpu.VMEM
    full = (X, BLK, WIDTH)
    four = (Y, X, BLK, 128)
    pair = (Y, 2, BLK, 128)
    blocks = (NBLK, BLK, 128)
    layer_out, grad_features, wg = pl.pallas_call(
        layer_kernel,
        out_shape=(sds((BLK, WIDTH), BF), sds((BLK, WIDTH), BF), sds((64, 256), F32)),
        in_specs=[SM] + [VM] * 7,
        out_specs=(VM,) * 3,
        scratch_shapes=[
            v(full, BF), v(full, BF), v((Y, 128, WIDTH), BF), v((Y, 128, WIDTH), BF),
            v((X, WIDTH, BLK), BF), v((X, WIDTH, BLK), BF),
            v((PARTS, 8, 128), F32), v((8, 128), jnp.int32), pltpu.SMEM((8, 128), jnp.int32),
            v(four, BF), v(four, BF), v(four, BF), v(four, BF),
            v((15, CAP, BLK, 128), BF), v((PARTS * CAP, BLK, 128), BF),
            v((15, CAP, BLK, 128), BF), v((PARTS * CAP, BLK, 128), BF),
            v((NBLK // 2, 4, GROUP, CHUNK), BF), v((4, GROUP, CHUNK), F32), v((4, 128, CHUNK), BF),
            v(blocks, BF), v(blocks, F32), v(blocks, F32), v(blocks, F32), v(blocks, F32),
            v(blocks, F32), v(blocks, F32),
            v(blocks, F32), v(blocks, BF), v((30, 128, BLK), F32), v(four, BF),
            v(pair, BF), v(pair, BF), v(four, BF), v(pair, BF), v(pair, BF),
            v((X, 2, BLK, WIDTH), BF), v((3, 2, BLK, WIDTH), BF), v((2,) + four, BF),
            v((2, Y, Z, 2, 64, 128), F32), v((2, Y, Z, 64, 128), BF), v((2, Y, Z, 64, 128), BF),
            v((2, 3, Z, 64, 128), BF), v((2, 3, Z, 64, 128), BF),
            v((2, Z, 64, 128), F32), v((2, Z, 64, 128), BF), v((2, 7, 64, 128), BF),
            pltpu.SemaphoreType.DMA((COPIES,)), pltpu.SemaphoreType.DMA((COPIES,)),
            pltpu.SemaphoreType.DMA,
        ],
        compiler_params=params(1),
        name="layer",
    )(tab, features, cotangent, w_key.T, w_value.T, w_query.T, w_output, req)
    return (
        layer_out,
        grad_features,
        wg[:, 128:192],
        wg[:, 0:64],
        wg[:, 64:128],
        wg[:, 192:256],
    )


def solution(mesh):
    return jax.shard_map(
        local,
        mesh=mesh,
        in_specs=(
            P(("dom", "head"), None),
            P(None, "head"),
            P(None, "head"),
            P(None, "head"),
            P("head", None),
            P(("dom", "head"), None),
            P("dom", None),
            P("dom", None),
            P("dom"),
        ),
        out_specs=(
            P(("dom", "head"), None),
            P(("dom", "head"), None),
            P("dom", "head"),
            P("dom", "head"),
            P("dom", "head"),
            P("dom", "head"),
        ),
        check_vma=False,
    )
```

time: 194 us -> 133 us (0.69)
  Pallas kernels: 177 us -> 124 us
  local copies, waits for them, and re-layouts: 11.4 us -> 5.24 us
    pallas_call x4 -> x1, Pallas kernels: 177 us -> 124 us  [local(): pl.pallas_call(layer_kernel, out_shape=(sds((BLK, WIDTH), BF), sds((BLK,...]
    unnamed x6 -> x10, local copies, waits for them, and re-layouts: 7.64 us -> 2.87 us
where the time goes in v2:
time: 133 us
  Pallas kernels  124 us (93%)
  local copies, waits for them, and re-layouts  5.24 us (4%)
  other arithmetic  1.76 us (1%)
  between operations  1.33 us (1%)
    pallas_call x1, Pallas kernels, local(): pl.pallas_call(layer_kernel, out_shape=(sds((BLK, WIDTH), BF), sds((BLK,...  124 us
    unnamed x10, local copies, waits for them, and re-layouts  2.87 us

profile of v2, /device:TPU:1, one launch (start us, length us, event | category | flops | bytes accessed | tf_op | source)
XLA Modules:
  0.0 132.7 jit_solution(16220801307690723446)
XLA Ops:
  0.6 0.7 fusion.8
  1.3 0.0 copy-start.3
  1.3 0.6 copy-done.3
  2.0 0.0 copy-start.2
  2.0 0.2 convert_reduce_fusion.2
  2.2 0.5 copy-done.2
  3.3 0.1 select_reduce_fusion.2
  3.4 0.1 select_reduce_fusion.1
  3.5 0.6 pad_add_fusion.tab
  4.1 0.1 select_reduce_fusion
  4.2 0.1 convert_element_type.23
  4.3 0.7 broadcast_in_dim.64.req
  5.0 124.4 %layer.1 = (bf16[128,1024]{1,0:T(8,128)(2,1)}, bf16[128,1024]{1,0:T(8,128)(2,1)}, f32[64,256]{1,0:T(8,128)}) custom-call(s32[96]{0:T(128)} %pad_add_fusion.tab, bf16[128,1024]{1,0:T(8,128)(2,1)} %feat.1, bf16[128,1024]{1,0:T(8,128)(2,1)} %cot.1, bf16[64,1024]{1,0:T(8,128)(2,1)} %bitcast.35, bf16[64,1024]{1,0:T(8,128)(2,1)} %bitcast.36, ...), custom_call_target="tpu_custom_call" | custom-call | tf_op jit(solution)/shard_map/layer/pallas_call | solution.py:511
  129.4 0.0 copy-start.1
  129.4 1.6 %fusion.10 = (f32[64,64]{1,0:T(8,128)}, f32[64,64]{1,0:T(8,128)}, f32[64,64]{1,0:T(8,128)}, f32[64,64]{1,0:T(8,128)}) fusion(f32[64,256]{1,0:T(8,128)} %get-tuple-element.11), kind=kLoop, calls=%fused_computation.49 | loop fusion | bytes 131072 | tf_op jit(solution)/shard_map/slice | solution.py:544
  130.9 0.0 copy-done.1
  130.9 0.0 copy-start
  131.0 0.7 copy.18
  131.7 0.3 copy-done
  132.0 0.7 copy.19
  (5 shorter events, 0.0 us)
Async XLA Ops:
  1.3 0.7 copy-start.3
  2.0 0.7 copy-start.2
  129.4 1.6 %copy-start.1 = (bf16[128,1024]{1,0:T(8,128)(2,1)S(1)}, bf16[128,1024]{1,0:T(8,128)(2,1)}, u32[]{:S(2)}) copy-start(bf16[128,1024]{1,0:T(8,128)(2,1)} %get-tuple-element.30) | copy-start | bytes 786436
  130.9 1.0 copy-start

commit v3 on v2

--- a/solution.py
+++ b/solution.py
@@ -36,15 +36,20 @@
     return d, lax.div(h, Y), lax.rem(h, Y)
 
 
-def greet(peers):
+def greet(peers, meanwhile):
     barrier = pltpu.get_barrier_semaphore()
     for peer in peers:
         pl.semaphore_signal(barrier, inc=1, device_id=peer, device_id_type=MESH)
+    meanwhile()
     pl.semaphore_wait(barrier, len(peers))
 
 
 def lanes(shape):
     return lax.broadcasted_iota(jnp.int32, shape, len(shape) - 1)
+
+
+def turned(t):
+    return lax.rem(t, 4) * 4 + lax.div(t, 4)
 
 
 class Sems:
@@ -60,6 +65,33 @@
         self.n += 1
         self.all.append(c)
         return c
+
+
+def slot_tables(source, target, count, req, table):
+    sub = lax.broadcasted_iota(jnp.int32, (128, 128), 0)
+    row = lax.broadcasted_iota(jnp.int32, (8, 128), 0)
+    lane = lax.broadcasted_iota(jnp.int32, (8, 128), 1)
+    ask = jnp.zeros((128, 128), jnp.int32)
+    tab = jnp.zeros((8, 128), jnp.int32)
+    owners = []
+    for j in range(16):
+        src, tgt = source[0, j], target[0, j]
+        owner, block = lax.div(src, NBLK), lax.rem(src, NBLK)
+        position = jnp.int32(0)
+        for o in owners:
+            position = position + jnp.where(o == owner, 1, 0)
+        owners.append(owner)
+        position = jnp.minimum(position, CAP - 1)
+        ask = ask + jnp.where(sub == owner * 8 + position, turned(block), 0)
+        slot, pos = owner * CAP + position, turned(tgt)
+        live = jnp.where(count[0] > j, 1, 0)
+        here, there = lane == pos, lane == slot
+        tab = tab + jnp.where((row == 0) & here, slot * live, 0)
+        tab = tab + jnp.where((row == 1) & here, live, 0)
+        tab = tab + jnp.where((row == 2) & there, pos * live, 0)
+        tab = tab + jnp.where((row == 3) & there, live, 0)
+    req[...] = ask.astype(F32).reshape(PARTS, 8, 128)
+    table[...] = tab
 
 
 def order_tables(asked, table):
@@ -87,12 +119,12 @@
 
 
 def layer_kernel(
-    tab, feat, cot, wk, wv, wq, wo, req,
+    source, target, count, feat, cot, wk, wv, wq, wo,
     lo, gf, wg,
-    feat_all, cot_all, wkv, wqo, feat_t, cot_t, asked, table, smem, kst, qst, kv_l, qg_l,
-    outgoing, incoming, sending, returned, probs, scores, kvt, qd, accq, outl, mrow, lrow, rl_s, rd_s,
-    dkv, egrad, runs, gkv, attp, gqp, g_kv, at_l, gq_l, part, rs, g2, wgf, sibs, sibr, ysend, yrecv,
-    own, zsend, zrecv, send_sems, recv_sems, local_sem,
+    req, tab_v, tab, feat_all, cot_all, wkv, wqo, feat_t, cot_t, asked, table, smem, kst, qst, kv_l, qg_l,
+    outgoing, incoming, sending, returned, probs, scores, kvt, qd, outl, mrow, lrow, rl_s, rd_s,
+    dkv, egrad, dses, qdt, runs, gkv, attp, gqp, g_kv, at_l, gq_l, part, gfq, rs, g2, wgf, sibs, sibr, ysend, yrecv,
+    own, zsend, zrecv, send_sems, recv_sems, local_sem, tab_sem,
 ):
     d, x, y = place()
     core, z = lax.rem(d, 2), lax.div(d, 2)
@@ -106,16 +138,25 @@
     up, down, yopp = dev(d, x, yp), dev(d, x, ym), dev(d, x, y2)
     doms = [lax.rem(d + k, PARTS) for k in range(1, PARTS)]
     sibling = dev(d + 1 - 2 * core, x, y)
-    greet([right, left, xopp, up, down, yopp] + [dev(q, x, y) for q in doms])
+
+    def prepare():
+        slot_tables(source, target, count, req, tab_v)
+        for w, o in ((wkv, (wk, wv)), (wqo, (wq, wo))):
+            w[y, 0:HD] = o[0][...]
+            w[y, HD:128] = o[1][...]
+        asked[d] = jnp.full((8, 128), 99.0, F32)
+        feat_all[x] = feat[...]
+        cot_all[x] = cot[...]
+
+    greet([right, left, xopp, up, down, yopp] + [dev(q, x, y) for q in doms], prepare)
+    tp = pltpu.make_async_copy(tab_v, tab, tab_sem)
+    tp.start()
     net = Sems(send_sems, recv_sems)
     start = net.start
     ysteps = [(y2, yopp), (yp, up), (ym, down)]
 
     fl = start(feat, feat_all.at[x], right)
     fr = start(feat, feat_all.at[x], left)
-    for i, (w, o) in enumerate(((wkv, (wk, wv)), (wqo, (wq, wo)))):
-        w[y, 0:HD] = o[0][...]
-        w[y, HD:128] = o[1][...]
     mine = pl.multiple_of(core * HD, HD)
     whole = pl.ds(mine, HD)
     upper, lower = pl.ds(mine, 32), pl.ds(mine + 32, 32)
@@ -124,9 +165,6 @@
         piece = w.at[y, whole]
         wown.append((start(piece, piece, up), start(piece, piece, down)))
     tables = [start(req.at[q], asked.at[d], dev(q, x, y)) for q in doms]
-    asked[d] = jnp.full((8, 128), 99.0, F32)
-    feat_all[x] = feat[...]
-    cot_all[x] = cot[...]
 
     def wmiddle(i):
         w = (wkv, wqo)[i]
@@ -164,8 +202,6 @@
 
     mkv = wmiddle(0)
     ffwd = xmiddle(feat_all, fl, fr)
-    cl = start(cot, cot_all.at[x], right)
-    cr = start(cot, cot_all.at[x], left)
     mqo = wmiddle(1)
     wlast(0, mkv)
     low4 = (lanes((BLK, 512)) & 127) < HD
@@ -185,9 +221,6 @@
         qg_l[y, b] = qst[y, b]
         return [start(qst.at[yy, b], qg_l.at[y, b], to) for yy, to in ysteps]
 
-    def turn(full, b, out):
-        out[b] = jnp.transpose(full[b])
-
     kvs = project_kv(x)
     kvs += project_kv(xm)
     kvs += project_kv(xp)
@@ -198,13 +231,12 @@
     cp.start()
     for c in ffwd:
         c.wait_recv()
+    cl = start(cot, cot_all.at[x], right)
+    cr = start(cot, cot_all.at[x], left)
     kvs += project_kv(x2)
     wlast(1, mqo)
-    qgs = project_qo(x)
-    cfwd = xmiddle(cot_all, cl, cr)
-    qgs += project_qo(xm)
-    qgs += project_qo(xp)
     cp.wait()
+    tp.wait()
     for c in kvs:
         c.wait_recv()
 
@@ -214,14 +246,18 @@
             at = jnp.clip(smem[0, q * 8 + c], 0, NBLK - 1)
             outgoing[k, c] = kv_l[lax.div(at, 4), lax.rem(at, 4)]
         going.append(start(outgoing.at[k], incoming.at[pl.ds(d * CAP, CAP)], dev(q, x, y)))
+    qgs = project_qo(x)
+    cfwd = xmiddle(cot_all, cl, cr)
+    qgs += project_qo(xm)
+    qgs += project_qo(xp)
     for c in cfwd:
         c.wait_recv()
     qgs += project_qo(x2)
     incoming[pl.ds(d * CAP, CAP)] = jnp.zeros((CAP, BLK, 128), BF)
     returned[pl.ds(d * CAP, CAP)] = jnp.zeros((CAP, BLK, 128), BF)
     for b in range(X):
-        turn(feat_all, b, feat_t)
-        turn(cot_all, b, cot_t)
+        feat_t[:, b * BLK : (b + 1) * BLK] = jnp.transpose(feat_all[b])
+        cot_t[:, b * BLK : (b + 1) * BLK] = jnp.transpose(cot_all[b])
     low1 = lanes((BLK, 128)) < HD
     low2 = lanes((GROUP, 128)) < HD
     for s in range(NBLK):
@@ -230,7 +266,9 @@
         c.wait_recv()
     for s in range(NBLK):
         p = qg_l[s // 4, s % 4]
-        qd[s] = jnp.where(low1, p * 0.125, p)
+        p = jnp.where(low1, p * 0.125, p)
+        qd[s] = p
+        qdt[s] = jnp.transpose(p)
     dkv[...] = jnp.zeros_like(dkv)
 
     nchunk = NBLK * BLK // CHUNK
@@ -270,47 +308,55 @@
     for c in going:
         c.wait_recv()
 
-    def extra(s):
-        blk = qd[s]
-        zero = jnp.zeros_like(blk)
-        ekv = incoming[tab[s]]
-        se = mm_nt(jnp.where(low1, blk, zero), ekv)
-        se = jnp.where(tab[NBLK + s] > 0, se, NEG_FILL)
-        ml, ll = mrow[s], lrow[s]
-        big = jnp.maximum(ml, jnp.max(se, 1, keepdims=True))
-        c = jnp.exp(ml - big)
-        ee = jnp.exp(se - big)
-        l = c * ll + jnp.sum(ee, 1, keepdims=True)
-        r = 1.0 / l
-        pe = ee * r
-        peb = pe.astype(BF)
-        rl = c * r
-        out = (outl[s] * rl + mm(peb, ekv)).astype(BF).astype(F32)
-        go = jnp.where(low1, zero, blk)
-        delta = jnp.sum(go.astype(F32) * out, 1, keepdims=True)
-        dse = (pe * (mm_nt(go, ekv) - delta)).astype(BF)
-        accq[s] = mm(dse, ekv)
-        rl_s[s] = rl
-        rd_s[s] = rl * delta
-        bt = jnp.transpose(blk)
-        egrad[s, 0:HD] = mm(bt[0:HD], dse).astype(BF)
-        egrad[s, HD:128] = mm(bt[HD:128], peb).astype(BF)
-        return out
+    batch = 8
 
     def extras(g, _):
-        a, b = extra(2 * g), extra(2 * g + 1)
-        attp[lax.div(g, 2), lax.rem(g, 2)] = jnp.where(low1, pltpu.roll(a, HD, 1), b).astype(BF)
+        ids = [batch * g + i for i in range(batch)]
+        blks = [qd[i] for i in ids]
+        ekvs = [incoming[jnp.clip(tab[0, i], 0, PARTS * CAP - 1)] for i in ids]
+        zero = jnp.zeros((BLK, 128), BF)
+        ses = [mm_nt(jnp.where(low1, b, zero), e) for b, e in zip(blks, ekvs)]
+        gos = [jnp.where(low1, zero, b) for b in blks]
+        dps = [mm_nt(o, e) for o, e in zip(gos, ekvs)]
+        ses = [jnp.where(tab[1, i] > 0, e, NEG_FILL) for i, e in zip(ids, ses)]
+        mls = [mrow[i] for i in ids]
+        bigs = [jnp.maximum(m, jnp.max(e, 1, keepdims=True)) for m, e in zip(mls, ses)]
+        cs = [jnp.exp(m - b) for m, b in zip(mls, bigs)]
+        ees = [jnp.exp(e - b) for e, b in zip(ses, bigs)]
+        ls = [c * lrow[i] + jnp.sum(e, 1, keepdims=True) for c, i, e in zip(cs, ids, ees)]
+        rs_ = [1.0 / v for v in ls]
+        pes = [e * r for e, r in zip(ees, rs_)]
+        pbs = [p.astype(BF) for p in pes]
+        rls = [c * r for c, r in zip(cs, rs_)]
+        outs = [
+            (outl[i] * r + mm(p, e)).astype(BF).astype(F32)
+            for i, r, p, e in zip(ids, rls, pbs, ekvs)
+        ]
+        deltas = [
+            jnp.sum(o.astype(F32) * a, 1, keepdims=True) for o, a in zip(gos, outs)
+        ]
+        dss = [(p * (dp - dl)).astype(BF) for p, dp, dl in zip(pes, dps, deltas)]
+        for n, i in enumerate(ids):
+            bt = qdt[i]
+            egrad[i, 0:HD] = mm(bt[0:HD], dss[n]).astype(BF)
+            egrad[i, HD:128] = mm(bt[HD:128], pbs[n]).astype(BF)
+        for n, i in enumerate(ids):
+            dses[i] = dss[n]
+            rl_s[i] = rls[n]
+            rd_s[i] = rls[n] * deltas[n]
+        for n in range(0, batch, 2):
+            attp[(batch // 4) * g + n // 4, (n // 2) % 2] = jnp.where(
+                low1, pltpu.roll(outs[n], HD, 1), outs[n + 1]
+            ).astype(BF)
         return 0
 
-    lax.fori_loop(0, NBLK // 2, extras, 0)
+    lax.fori_loop(0, NBLK // batch, extras, 0)
     home = []
     for k, q in enumerate(doms):
         for c in range(CAP):
             slot = q * CAP + c
-            got = egrad[tab[2 * NBLK + slot]]
-            sending[k, c] = jnp.where(
-                tab[2 * NBLK + PARTS * CAP + slot] > 0, got, jnp.zeros_like(got)
-            )
+            got = egrad[jnp.clip(tab[2, slot], 0, NBLK - 1)]
+            sending[k, c] = jnp.where(tab[3, slot] > 0, got, jnp.zeros_like(got))
         home.append(start(sending.at[k], returned.at[pl.ds(d * CAP, CAP)], dev(q, x, y)))
     ats = [start(attp.at[yy], at_l.at[y], to) for yy, to in ysteps]
     at_l[y] = attp[y]
@@ -322,7 +368,13 @@
         zz = jnp.where(low2, p, (p.astype(F32) * rl).astype(BF))
         zt = jnp.transpose(zz)
         go = jnp.where(low2, jnp.zeros_like(zz), zz)
-        dq = accq[pl.ds(2 * g, 2)].reshape(GROUP, 128)
+        dq = jnp.concatenate(
+            [
+                mm(dses[2 * g + i], incoming[jnp.clip(tab[0, 2 * g + i], 0, PARTS * CAP - 1)])
+                for i in range(2)
+            ],
+            0,
+        )
         for c in range(nchunk):
             dp = mm(go, kvt[c])
             eb = probs[g, c]
@@ -343,6 +395,9 @@
     gqs = [start(gqp.at[yy], gq_l.at[y], to) for yy, to in ysteps]
     gq_l[y] = gqp[y]
 
+    def two(ref, h):
+        return jnp.concatenate([ref[h].reshape(rows, 128), ref[h + 1].reshape(rows, 128)], 1)
+
     rows = X * BLK
     for c in ats:
         c.wait_recv()
@@ -355,24 +410,20 @@
     for n in range(4):
         cols = pl.ds(n * 256, 256)
         o = None
-        for h in range(Y):
-            t = mm(g2[1, h].reshape(rows, 128), wqo[h, :, cols])
+        for h in range(0, Y, 2):
+            t = mm(two(g2.at[1], h), wqo[h : h + 2, :, cols].reshape(256, 256))
             o = t if o is None else o + t
         part[:, 0, :, cols] = o.astype(BF).reshape(X, BLK, 256)
     xsteps = [(x2, xopp), (xp, right), (xm, left)]
     los = [start(part.at[xx, 0], rs.at[k, 0], to) for k, (xx, to) in enumerate(xsteps)]
 
-    def tmm(t, g):
-        r = None
-        for b in range(X):
-            v = mm(t[b], g[b])
-            r = v if r is None else r + v
-        return r
-
     def weights(i, left_of):
         out = []
         for h in range(Y):
-            wgf[i, h] = left_of(h).reshape(Z, 2, 64, 128)
+            if h % 2 == 0:
+                both = left_of(h)
+                for j in range(2):
+                    wgf[i, h + j] = both[:, j * 128 : (j + 1) * 128].reshape(Z, 2, 64, 128)
             sibs[i, h] = wgf[i, h, :, 1 - core].astype(BF)
             out.append(start(sibs.at[i, h], sibr.at[i, h], sibling))
         return out
@@ -415,8 +466,15 @@
             zero = jnp.zeros_like(p)
             g2[0, h, 2 * j] = jnp.where(low1, p, zero).astype(BF)
             g2[0, h, 2 * j + 1] = jnp.where(low1, pltpu.roll(p, HD, 1), zero).astype(BF)
-    sib1 = weights(1, lambda h: tmm(feat_t, g2[0, h]) + tmm(cot_t, g2[1, h]))
+    sib1 = weights(1, lambda h: mm(feat_t[...], two(g2.at[0], h)) + mm(cot_t[...], two(g2.at[1], h)))
     y1 = along_y(1, sib1)
+    for n in range(4):
+        cols = pl.ds(n * 256, 256)
+        o = None
+        for h in range(0, Y, 2):
+            t = mm(two(g2.at[0], h), wqo[h : h + 2, :, cols].reshape(256, 256))
+            o = t if o is None else o + t
+        gfq[:, cols] = o
     for c in home:
         c.wait_recv()
     running = None
@@ -425,23 +483,25 @@
         running = got if k == 0 else got + running * smem[2, k].astype(F32)
         runs[k] = running
     for s in range(NBLK):
-        more = jnp.where(smem[4, s] > 0, runs[jnp.clip(smem[3, s], 0, CAP * (PARTS - 1) - 1)], jnp.zeros((128, BLK), F32))
+        more = jnp.where(
+            smem[4, s] > 0,
+            runs[jnp.clip(smem[3, s], 0, CAP * (PARTS - 1) - 1)],
+            jnp.zeros((128, BLK), F32),
+        )
         gkv[s // 4, s % 4] = jnp.transpose(dkv[s] + more).astype(BF)
     gks = [start(gkv.at[yy], g_kv.at[y], to) for yy, to in ysteps]
     g_kv[y] = gkv[y]
     z1 = along_z(1, y1)
     for c in gks:
         c.wait_recv()
+    sib0 = weights(0, lambda h: mm(feat_t[...], two(g_kv, h)))
     for n in range(4):
         cols = pl.ds(n * 256, 256)
-        o = None
-        for h in range(Y):
-            t = mm(g2[0, h].reshape(rows, 128), wqo[h, :, cols])
-            t = t + mm(g_kv[h].reshape(rows, 128), wkv[h, :, cols])
-            o = t if o is None else o + t
+        o = gfq[:, cols]
+        for h in range(0, Y, 2):
+            o = o + mm(two(g_kv, h), wkv[h : h + 2, :, cols].reshape(256, 256))
         part[:, 1, :, cols] = o.astype(BF).reshape(X, BLK, 256)
     gfs = [start(part.at[xx, 1], rs.at[k, 1], to) for k, (xx, to) in enumerate(xsteps)]
-    sib0 = weights(0, lambda h: tmm(feat_t, g_kv[h]))
     y0 = along_y(0, sib0)
     for i, (copies, base, out) in enumerate(((los, feat, lo), (gfs, cot, gf))):
         if i == 1:
@@ -457,6 +517,13 @@
         c.wait_send()
 
 
+def hand_over_kernel(lo, gf, wg, lo_o, gf_o, q_o, k_o, v_o, o_o):
+    lo_o[...] = lo[...]
+    gf_o[...] = gf[...]
+    for i, o in enumerate((k_o, v_o, q_o, o_o)):
+        o[...] = wg[:, i * HD : (i + 1) * HD]
+
+
 VM = pl.BlockSpec(memory_space=pltpu.VMEM)
 SM = pl.BlockSpec(memory_space=pltpu.SMEM)
 COPIES = 134
@@ -472,37 +539,9 @@
     )
 
 
-def turned(t):
-    return (t % 4) * 4 + t // 4
-
-
 def local(
     features, w_query, w_key, w_value, w_output, cotangent, cross_source, cross_target, cross_count
 ):
-    source, target, live_count = cross_source[0], cross_target[0], cross_count[0]
-    owners = source // NBLK
-    slot_ids = jnp.arange(16, dtype=jnp.int32)
-    earlier = (owners[:, None] == owners[None, :]) & (slot_ids[None, :] < slot_ids[:, None])
-    position = jnp.sum(earlier.astype(jnp.int32), 1)
-    slot = owners * CAP + position
-    placed = slot[:, None] == jnp.arange(PARTS * CAP, dtype=jnp.int32)[None, :]
-    live = slot_ids < live_count
-    row_slot = jnp.arange(PARTS * 8, dtype=jnp.int32)
-    row_slot = jnp.where(row_slot % 8 < CAP, (row_slot // 8) * CAP + row_slot % 8, -1)
-    placed_row = slot[:, None] == row_slot[None, :]
-    request = jnp.sum(jnp.where(placed_row, turned(source % NBLK)[:, None], 0), 0)
-    req = jnp.broadcast_to(request.astype(F32).reshape(PARTS, 8, 1), (PARTS, 8, 128))
-    tpos = turned(target)
-    chosen = (tpos[:, None] == slot_ids[None, :]) & live[:, None]
-    alive = placed & live[:, None]
-    tab = jnp.concatenate(
-        [
-            jnp.sum(jnp.where(chosen, slot[:, None], 0), 0),
-            jnp.sum(chosen.astype(jnp.int32), 0),
-            jnp.sum(jnp.where(alive, tpos[:, None], 0), 0),
-            jnp.sum(alive.astype(jnp.int32), 0),
-        ]
-    )
     v = pltpu.VMEM
     full = (X, BLK, WIDTH)
     four = (Y, X, BLK, 128)
@@ -511,38 +550,42 @@
     layer_out, grad_features, wg = pl.pallas_call(
         layer_kernel,
         out_shape=(sds((BLK, WIDTH), BF), sds((BLK, WIDTH), BF), sds((64, 256), F32)),
-        in_specs=[SM] + [VM] * 7,
+        in_specs=[SM] * 3 + [VM] * 6,
         out_specs=(VM,) * 3,
         scratch_shapes=[
+            v((PARTS, 8, 128), F32), v((8, 128), jnp.int32), pltpu.SMEM((8, 128), jnp.int32),
             v(full, BF), v(full, BF), v((Y, 128, WIDTH), BF), v((Y, 128, WIDTH), BF),
-            v((X, WIDTH, BLK), BF), v((X, WIDTH, BLK), BF),
+            v((WIDTH, X * BLK), BF), v((WIDTH, X * BLK), BF),
             v((PARTS, 8, 128), F32), v((8, 128), jnp.int32), pltpu.SMEM((8, 128), jnp.int32),
             v(four, BF), v(four, BF), v(four, BF), v(four, BF),
             v((15, CAP, BLK, 128), BF), v((PARTS * CAP, BLK, 128), BF),
             v((15, CAP, BLK, 128), BF), v((PARTS * CAP, BLK, 128), BF),
             v((NBLK // 2, 4, GROUP, CHUNK), BF), v((4, GROUP, CHUNK), F32), v((4, 128, CHUNK), BF),
             v(blocks, BF), v(blocks, F32), v(blocks, F32), v(blocks, F32), v(blocks, F32),
-            v(blocks, F32), v(blocks, F32),
-            v(blocks, F32), v(blocks, BF), v((30, 128, BLK), F32), v(four, BF),
+            v(blocks, F32),
+            v(blocks, F32), v(blocks, BF), v(blocks, BF), v(blocks, BF), v((30, 128, BLK), F32), v(four, BF),
             v(pair, BF), v(pair, BF), v(four, BF), v(pair, BF), v(pair, BF),
-            v((X, 2, BLK, WIDTH), BF), v((3, 2, BLK, WIDTH), BF), v((2,) + four, BF),
+            v((X, 2, BLK, WIDTH), BF), v((X * BLK, WIDTH), F32), v((3, 2, BLK, WIDTH), BF), v((2,) + four, BF),
             v((2, Y, Z, 2, 64, 128), F32), v((2, Y, Z, 64, 128), BF), v((2, Y, Z, 64, 128), BF),
             v((2, 3, Z, 64, 128), BF), v((2, 3, Z, 64, 128), BF),
             v((2, Z, 64, 128), F32), v((2, Z, 64, 128), BF), v((2, 7, 64, 128), BF),
             pltpu.SemaphoreType.DMA((COPIES,)), pltpu.SemaphoreType.DMA((COPIES,)),
-            pltpu.SemaphoreType.DMA,
+            pltpu.SemaphoreType.DMA, pltpu.SemaphoreType.DMA,
         ],
         compiler_params=params(1),
         name="layer",
-    )(tab, features, cotangent, w_key.T, w_value.T, w_query.T, w_output, req)
-    return (
-        layer_out,
-        grad_features,
-        wg[:, 128:192],
-        wg[:, 0:64],
-        wg[:, 64:128],
-        wg[:, 192:256],
+    )(
+        cross_source, cross_target, cross_count, features, cotangent,
+        w_key.T, w_value.T, w_query.T, w_output,
     )
+    square = sds((HD, HD), F32)
+    return pl.pallas_call(
+        hand_over_kernel,
+        out_shape=(sds((BLK, WIDTH), BF), sds((BLK, WIDTH), BF), square, square, square, square),
+        in_specs=[VM] * 3,
+        out_specs=(VM,) * 6,
+        name="hand_over",
+    )(layer_out, grad_features, wg)
 
 
 def solution(mesh):

time: 133 us -> 114 us (0.86)
  Pallas kernels: 124 us -> 112 us
  local copies, waits for them, and re-layouts: 5.24 us -> 0 us
  other arithmetic: 1.76 us -> 0 us
    pallas_call x1, Pallas kernels: 124 us -> 110 us  [local(): pl.pallas_call(layer_kernel, out_shape=(sds((BLK, WIDTH), BF), sds((BLK,...]
    unnamed x10 -> x0, local copies, waits for them, and re-layouts: 2.87 us -> none
    pallas_call x0 -> x1, Pallas kernels: none -> 1.87 us  [local(): pl.pallas_call(hand_over_kernel, out_shape=(sds((BLK, WIDTH), BF), sds((B...]
    slice x1 -> x0, local copies, waits for them, and re-layouts: 1.57 us -> none  [local(): wg[:, 192:256]]
where the time goes in v3:
time: 114 us; the launch traced here: 113 us
  Pallas kernels  112 us (98%)
  between operations  1.29 us (1%)
    pallas_call x1, Pallas kernels, local(): pl.pallas_call(layer_kernel, out_shape=(sds((BLK, WIDTH), BF), sds((BLK,...  110 us

profile of v3, /device:TPU:1, one launch (start us, length us, event | category | flops | bytes accessed | tf_op | source)
XLA Modules:
  0.0 113.5 jit_solution(826522887827456624)
XLA Ops:
  1.3 110.3 %layer.1 = (bf16[128,1024]{1,0:T(8,128)(2,1)}, bf16[128,1024]{1,0:T(8,128)(2,1)}, f32[64,256]{1,0:T(8,128)}) custom-call(s32[1,16]{1,0:T(1,128)} %source.1, s32[1,16]{1,0:T(1,128)} %target.1, s32[1]{0:T(128)S(6)} %copy.15.count, bf16[128,1024]{1,0:T(8,128)(2,1)} %feat.1, bf16[128,1024]{1,0:T(8,128)(2,1)} %cot.1, bf16[64,1024]{1,0:T(8,128)(2,1)} %bitcast.3, ...), custom_call_target="tpu_custom_call" | custom-call | tf_op jit(solution)/shard_map/layer/pallas_call | solution.py:550
  111.6 1.9 %hand_over.1 = (bf16[128,1024]{1,0:T(8,128)(2,1)}, bf16[128,1024]{1,0:T(8,128)(2,1)}, f32[64,64]{1,0:T(8,128)}, f32[64,64]{1,0:T(8,128)}, f32[64,64]{1,0:T(8,128)}, /*index=5*/f32[64,64]{1,0:T(8,128)}) custom-call(bf16[128,1024]{1,0:T(8,128)(2,1)} %get-tuple-element.9.lo, bf16[128,1024]{1,0:T(8,128)(2,1)} %get-tuple-element.10.gf, ...), custom_call_target="tpu_custom_call" | custom-call | tf_op jit(solution)/shard_map/hand_over/pallas_call | solution.py:582

commit v4 on v3

--- a/solution.py
+++ b/solution.py
@@ -65,6 +65,33 @@
         self.n += 1
         self.all.append(c)
         return c
+
+    def group(self, landing):
+        g = Group(self, self.n, landing)
+        self.n += 1
+        self.all.append(g)
+        return g
+
+
+class Group:
+    def __init__(self, net, n, landing):
+        self.net, self.n, self.landing, self.to = net, n, landing, None
+
+    def copy(self, src, dst, to):
+        return pltpu.make_async_remote_copy(
+            src_ref=src, dst_ref=dst, send_sem=self.net.send.at[self.n],
+            recv_sem=self.net.recv.at[self.n], device_id=to, device_id_type=MESH,
+        )
+
+    def start(self, src, dst, to):
+        self.to = to
+        self.copy(src, dst, to).start()
+
+    def wait_recv(self):
+        self.copy(self.landing, self.landing, self.to).wait_recv()
+
+    def wait_send(self):
+        self.copy(self.landing, self.landing, self.to).wait_send()
 
 
 def slot_tables(source, target, count, req, table):
@@ -155,8 +182,14 @@
     start = net.start
     ysteps = [(y2, yopp), (yp, up), (ym, down)]
 
-    fl = start(feat, feat_all.at[x], right)
-    fr = start(feat, feat_all.at[x], left)
+    def along_x(own_rows, full):
+        top, bottom = pl.ds(0, HD), pl.ds(HD, HD)
+        out = []
+        for first, second, to in ((top, bottom, right), (bottom, top, left)):
+            out.append([start(own_rows.at[h], full.at[x, h], to) for h in (first, second)])
+        return out
+
+    fx = along_x(feat, feat_all)
     mine = pl.multiple_of(core * HD, HD)
     whole = pl.ds(mine, HD)
     upper, lower = pl.ds(mine, 32), pl.ds(mine + 32, 32)
@@ -164,7 +197,9 @@
     for w in (wkv, wqo):
         piece = w.at[y, whole]
         wown.append((start(piece, piece, up), start(piece, piece, down)))
-    tables = [start(req.at[q], asked.at[d], dev(q, x, y)) for q in doms]
+    tables = net.group(asked.at[pl.ds(0, PARTS - 1)])
+    for q in doms:
+        tables.start(req.at[q], asked.at[d], dev(q, x, y))
 
     def wmiddle(i):
         w = (wkv, wqo)[i]
@@ -191,17 +226,20 @@
         mid[3].wait_recv()
         s3.wait_recv()
 
-    def xmiddle(full, a, b):
-        a.wait_recv()
+    def xmiddle(full, halves):
+        (a0, a1), (b0, b1) = halves
+        a0.wait_recv()
         p = full.at[xm, pl.ds(0, HD)]
         f1 = start(p, p, right)
-        b.wait_recv()
+        b0.wait_recv()
         p = full.at[xp, pl.ds(HD, HD)]
         f2 = start(p, p, left)
+        a1.wait_recv()
+        b1.wait_recv()
         return f1, f2
 
     mkv = wmiddle(0)
-    ffwd = xmiddle(feat_all, fl, fr)
+    ffwd = xmiddle(feat_all, fx)
     mqo = wmiddle(1)
     wlast(0, mkv)
     low4 = (lanes((BLK, 512)) & 127) < HD
@@ -211,7 +249,8 @@
         for h in range(Y):
             kst[h, b] = r[:, h * 128 : (h + 1) * 128]
         kv_l[y, b] = kst[y, b]
-        return [start(kst.at[yy, b], kv_l.at[y, b], to) for yy, to in ysteps]
+        for yy, to in ysteps:
+            kvs.start(kst.at[yy, b], kv_l.at[y, b], to)
 
     def project_qo(b):
         w = wqo[...].reshape(Y * 128, WIDTH)
@@ -219,40 +258,39 @@
         for h in range(Y):
             qst[h, b] = r[:, h * 128 : (h + 1) * 128]
         qg_l[y, b] = qst[y, b]
-        return [start(qst.at[yy, b], qg_l.at[y, b], to) for yy, to in ysteps]
-
-    kvs = project_kv(x)
-    kvs += project_kv(xm)
-    kvs += project_kv(xp)
-    for c in tables:
-        c.wait_recv()
+        for yy, to in ysteps:
+            qgs.start(qst.at[yy, b], qg_l.at[y, b], to)
+
+    kvs, qgs = net.group(kv_l.at[pl.ds(0, 3)]), net.group(qg_l.at[pl.ds(0, 3)])
+    project_kv(x)
+    project_kv(xm)
+    project_kv(xp)
+    tables.wait_recv()
     order_tables(asked, table)
     cp = pltpu.make_async_copy(table, smem, local_sem)
     cp.start()
     for c in ffwd:
         c.wait_recv()
-    cl = start(cot, cot_all.at[x], right)
-    cr = start(cot, cot_all.at[x], left)
-    kvs += project_kv(x2)
-    wlast(1, mqo)
+    cx = along_x(cot, cot_all)
+    project_kv(x2)
     cp.wait()
     tp.wait()
-    for c in kvs:
-        c.wait_recv()
-
-    going = []
+    kvs.wait_recv()
+
+    going = net.group(incoming.at[pl.ds(0, CAP * (PARTS - 1))])
     for k, q in enumerate(doms):
         for c in range(CAP):
             at = jnp.clip(smem[0, q * 8 + c], 0, NBLK - 1)
             outgoing[k, c] = kv_l[lax.div(at, 4), lax.rem(at, 4)]
-        going.append(start(outgoing.at[k], incoming.at[pl.ds(d * CAP, CAP)], dev(q, x, y)))
-    qgs = project_qo(x)
-    cfwd = xmiddle(cot_all, cl, cr)
-    qgs += project_qo(xm)
-    qgs += project_qo(xp)
+        going.start(outgoing.at[k], incoming.at[pl.ds(d * CAP, CAP)], dev(q, x, y))
+    wlast(1, mqo)
+    project_qo(x)
+    cfwd = xmiddle(cot_all, cx)
+    project_qo(xm)
+    project_qo(xp)
     for c in cfwd:
         c.wait_recv()
-    qgs += project_qo(x2)
+    project_qo(x2)
     incoming[pl.ds(d * CAP, CAP)] = jnp.zeros((CAP, BLK, 128), BF)
     returned[pl.ds(d * CAP, CAP)] = jnp.zeros((CAP, BLK, 128), BF)
     for b in range(X):
@@ -262,8 +300,7 @@
     low2 = lanes((GROUP, 128)) < HD
     for s in range(NBLK):
         kvt[s // 4, :, pl.ds((s % 4) * 128, 128)] = jnp.transpose(kv_l[s // 4, s % 4])
-    for c in qgs:
-        c.wait_recv()
+    qgs.wait_recv()
     for s in range(NBLK):
         p = qg_l[s // 4, s % 4]
         p = jnp.where(low1, p * 0.125, p)
@@ -305,8 +342,7 @@
         return 0
 
     lax.fori_loop(0, NBLK // 2, forward, 0)
-    for c in going:
-        c.wait_recv()
+    going.wait_recv()
 
     batch = 8
 
@@ -351,14 +387,16 @@
         return 0
 
     lax.fori_loop(0, NBLK // batch, extras, 0)
-    home = []
+    home = net.group(returned.at[pl.ds(0, CAP * (PARTS - 1))])
     for k, q in enumerate(doms):
         for c in range(CAP):
             slot = q * CAP + c
             got = egrad[jnp.clip(tab[2, slot], 0, NBLK - 1)]
             sending[k, c] = jnp.where(tab[3, slot] > 0, got, jnp.zeros_like(got))
-        home.append(start(sending.at[k], returned.at[pl.ds(d * CAP, CAP)], dev(q, x, y)))
-    ats = [start(attp.at[yy], at_l.at[y], to) for yy, to in ysteps]
+        home.start(sending.at[k], returned.at[pl.ds(d * CAP, CAP)], dev(q, x, y))
+    ats = net.group(at_l.at[pl.ds(0, 3)])
+    for yy, to in ysteps:
+        ats.start(attp.at[yy], at_l.at[y], to)
     at_l[y] = attp[y]
 
     def backward(g, _):
@@ -392,15 +430,17 @@
         return 0
 
     lax.fori_loop(0, NBLK // 2, backward, 0)
-    gqs = [start(gqp.at[yy], gq_l.at[y], to) for yy, to in ysteps]
+    gqs = net.group(gq_l.at[pl.ds(0, 3)])
+    for yy, to in ysteps:
+        gqs.start(gqp.at[yy], gq_l.at[y], to)
     gq_l[y] = gqp[y]
 
-    def two(ref, h):
-        return jnp.concatenate([ref[h].reshape(rows, 128), ref[h + 1].reshape(rows, 128)], 1)
+    def two(ref, h, h2=None):
+        h2 = h + 1 if h2 is None else h2
+        return jnp.concatenate([ref[h].reshape(rows, 128), ref[h2].reshape(rows, 128)], 1)
 
     rows = X * BLK
-    for c in ats:
-        c.wait_recv()
+    ats.wait_recv()
     for h in range(Y):
         for j in range(2):
             p = at_l[h, j].astype(F32)
@@ -415,58 +455,63 @@
             o = t if o is None else o + t
         part[:, 0, :, cols] = o.astype(BF).reshape(X, BLK, 256)
     xsteps = [(x2, xopp), (xp, right), (xm, left)]
-    los = [start(part.at[xx, 0], rs.at[k, 0], to) for k, (xx, to) in enumerate(xsteps)]
+    los, gfs = net.group(rs.at[:, 0]), net.group(rs.at[:, 1])
+    for k, (xx, to) in enumerate(xsteps):
+        los.start(part.at[xx, 0], rs.at[k, 0], to)
+
+    yorder = [yy for yy, _ in ysteps] + [y]
 
     def weights(i, left_of):
         out = []
-        for h in range(Y):
-            if h % 2 == 0:
-                both = left_of(h)
-                for j in range(2):
-                    wgf[i, h + j] = both[:, j * 128 : (j + 1) * 128].reshape(Z, 2, 64, 128)
-            sibs[i, h] = wgf[i, h, :, 1 - core].astype(BF)
-            out.append(start(sibs.at[i, h], sibr.at[i, h], sibling))
+        for n in (0, 2):
+            pick = yorder[n : n + 2]
+            both = left_of(*pick)
+            c = net.group(sibr.at[i, pl.ds(0, 2)])
+            for j, h in enumerate(pick):
+                wgf[i, h] = both[:, j * 128 : (j + 1) * 128].reshape(Z, 2, 64, 128)
+                sibs[i, h] = wgf[i, h, :, 1 - core].astype(BF)
+                c.start(sibs.at[i, h], sibr.at[i, h], sibling)
+            out.append(c)
         return out
 
     def along_y(i, sib):
-        for c in sib:
-            c.wait_recv()
-        out = []
+        out = net.group(yrecv.at[i])
         for k, (yy, to) in enumerate(ysteps):
+            if k != 1:
+                sib[k // 2].wait_recv()
             ysend[i, k] = (wgf[i, yy, :, core] + sibr[i, yy].astype(F32)).astype(BF)
-            out.append(start(ysend.at[i, k], yrecv.at[i, k], to))
+            out.start(ysend.at[i, k], yrecv.at[i, k], to)
         return out
 
     zsteps = [lax.rem(z + k, Z) for k in (4, 3, 5, 2, 6, 1, 7)]
 
     def along_z(i, ys):
         total = wgf[i, y, :, core] + sibr[i, y].astype(F32)
+        ys.wait_recv()
         for k in range(3):
-            ys[k].wait_recv()
             total = total + yrecv[i, k].astype(F32)
         own[i] = total
         zsend[i] = total.astype(BF)
-        return [
-            start(zsend.at[i, zz], zrecv.at[i, k], dev(zz * 2 + core, x, y))
-            for k, zz in enumerate(zsteps)
-        ]
+        out = net.group(zrecv.at[i])
+        for k, zz in enumerate(zsteps):
+            out.start(zsend.at[i, zz], zrecv.at[i, k], dev(zz * 2 + core, x, y))
+        return out
 
     def finish(i, zsum):
         res = own[i, z]
+        zsum.wait_recv()
         for k in range(7):
-            zsum[k].wait_recv()
             res = res + zrecv[i, k].astype(F32)
         wg[:, i * 128 : (i + 1) * 128] = res
 
-    for c in gqs:
-        c.wait_recv()
+    gqs.wait_recv()
     for h in range(Y):
         for j in range(2):
             p = gq_l[h, j].astype(F32)
             zero = jnp.zeros_like(p)
             g2[0, h, 2 * j] = jnp.where(low1, p, zero).astype(BF)
             g2[0, h, 2 * j + 1] = jnp.where(low1, pltpu.roll(p, HD, 1), zero).astype(BF)
-    sib1 = weights(1, lambda h: mm(feat_t[...], two(g2.at[0], h)) + mm(cot_t[...], two(g2.at[1], h)))
+    sib1 = weights(1, lambda h, h2: mm(feat_t[...], two(g2.at[0], h, h2)) + mm(cot_t[...], two(g2.at[1], h, h2)))
     y1 = along_y(1, sib1)
     for n in range(4):
         cols = pl.ds(n * 256, 256)
@@ -474,9 +519,8 @@
         for h in range(0, Y, 2):
             t = mm(two(g2.at[0], h), wqo[h : h + 2, :, cols].reshape(256, 256))
             o = t if o is None else o + t
-        gfq[:, cols] = o
-    for c in home:
-        c.wait_recv()
+        gfq[:, :, cols] = o.reshape(X, BLK, 256)
+    home.wait_recv()
     running = None
     for k in range(CAP * (PARTS - 1)):
         got = returned[jnp.clip(smem[1, k], 0, PARTS * CAP - 1)].astype(F32)
@@ -489,27 +533,38 @@
             jnp.zeros((128, BLK), F32),
         )
         gkv[s // 4, s % 4] = jnp.transpose(dkv[s] + more).astype(BF)
-    gks = [start(gkv.at[yy], g_kv.at[y], to) for yy, to in ysteps]
+    xorder = [(x2, xopp), (xp, right), (xm, left), (x, None)]
+    gks = []
+    for b, _ in xorder:
+        c = net.group(g_kv.at[pl.ds(0, 3), b])
+        for yy, to in ysteps:
+            c.start(gkv.at[yy, b], g_kv.at[y, b], to)
+        gks.append(c)
     g_kv[y] = gkv[y]
     z1 = along_z(1, y1)
-    for c in gks:
-        c.wait_recv()
-    sib0 = weights(0, lambda h: mm(feat_t[...], two(g_kv, h)))
-    for n in range(4):
-        cols = pl.ds(n * 256, 256)
-        o = gfq[:, cols]
+
+    def feature_part(b):
+        o = gfq[b]
         for h in range(0, Y, 2):
-            o = o + mm(two(g_kv, h), wkv[h : h + 2, :, cols].reshape(256, 256))
-        part[:, 1, :, cols] = o.astype(BF).reshape(X, BLK, 256)
-    gfs = [start(part.at[xx, 1], rs.at[k, 1], to) for k, (xx, to) in enumerate(xsteps)]
+            g = jnp.concatenate([g_kv[h, b], g_kv[h + 1, b]], 1)
+            o = o + mm(g, wkv[h : h + 2].reshape(256, WIDTH))
+        part[b, 1] = o.astype(BF)
+
+    for k, (b, to) in enumerate(xorder):
+        gks[k].wait_recv()
+        if k < 3:
+            feature_part(b)
+            gfs.start(part.at[b, 1], rs.at[k, 1], to)
+    sib0 = weights(0, lambda h, h2: mm(feat_t[...], two(g_kv, h, h2)))
+    feature_part(x)
     y0 = along_y(0, sib0)
     for i, (copies, base, out) in enumerate(((los, feat, lo), (gfs, cot, gf))):
         if i == 1:
             finish(1, z1)
             z0 = along_z(0, y0)
         total = part[x, i].astype(F32)
+        copies.wait_recv()
         for k in range(3):
-            copies[k].wait_recv()
             total = total + rs[k, i].astype(F32)
         out[...] = (base[...].astype(F32) + total).astype(BF)
     finish(0, z0)
@@ -526,7 +581,7 @@
 
 VM = pl.BlockSpec(memory_space=pltpu.VMEM)
 SM = pl.BlockSpec(memory_space=pltpu.SMEM)
-COPIES = 134
+COPIES = 47
 
 
 def sds(shape, dtype):
@@ -565,7 +620,7 @@
             v(blocks, F32),
             v(blocks, F32), v(blocks, BF), v(blocks, BF), v(blocks, BF), v((30, 128, BLK), F32), v(four, BF),
             v(pair, BF), v(pair, BF), v(four, BF), v(pair, BF), v(pair, BF),
-            v((X, 2, BLK, WIDTH), BF), v((X * BLK, WIDTH), F32), v((3, 2, BLK, WIDTH), BF), v((2,) + four, BF),
+            v((X, 2, BLK, WIDTH), BF), v((X, BLK, WIDTH), F32), v((3, 2, BLK, WIDTH), BF), v((2,) + four, BF),
             v((2, Y, Z, 2, 64, 128), F32), v((2, Y, Z, 64, 128), BF), v((2, Y, Z, 64, 128), BF),
             v((2, 3, Z, 64, 128), BF), v((2, 3, Z, 64, 128), BF),
             v((2, Z, 64, 128), F32), v((2, Z, 64, 128), BF), v((2, 7, 64, 128), BF),

time: 114 us -> 111 us (0.974)
  Pallas kernels: 112 us -> 110 us
    pallas_call x1, Pallas kernels: 110 us -> 108 us  [local(): pl.pallas_call(layer_kernel, out_shape=(sds((BLK, WIDTH), BF), sds((BLK,...]
where the time goes in v4:
time: 111 us
  Pallas kernels  110 us (99%)
  between operations  1.29 us (1%)
    pallas_call x1, Pallas kernels, local(): pl.pallas_call(layer_kernel, out_shape=(sds((BLK, WIDTH), BF), sds((BLK,...  108 us

profile of v4, /device:TPU:1, one launch (start us, length us, event | category | flops | bytes accessed | tf_op | source)
XLA Modules:
  0.0 110.9 jit_solution(6069842693456272055)
XLA Ops:
  1.3 107.7 %layer.1 = (bf16[128,1024]{1,0:T(8,128)(2,1)}, bf16[128,1024]{1,0:T(8,128)(2,1)}, f32[64,256]{1,0:T(8,128)}) custom-call(s32[1,16]{1,0:T(1,128)} %source.1, s32[1,16]{1,0:T(1,128)} %target.1, s32[1]{0:T(128)S(6)} %copy.15.count, bf16[128,1024]{1,0:T(8,128)(2,1)} %feat.1, bf16[128,1024]{1,0:T(8,128)(2,1)} %cot.1, bf16[64,1024]{1,0:T(8,128)(2,1)} %bitcast.3, ...), custom_call_target="tpu_custom_call" | custom-call | tf_op jit(solution)/shard_map/layer/pallas_call | solution.py:605
  109.0 1.9 %hand_over.1 = (bf16[128,1024]{1,0:T(8,128)(2,1)}, bf16[128,1024]{1,0:T(8,128)(2,1)}, f32[64,64]{1,0:T(8,128)}, f32[64,64]{1,0:T(8,128)}, f32[64,64]{1,0:T(8,128)}, /*index=5*/f32[64,64]{1,0:T(8,128)}) custom-call(bf16[128,1024]{1,0:T(8,128)(2,1)} %get-tuple-element.9.lo, bf16[128,1024]{1,0:T(8,128)(2,1)} %get-tuple-element.10.gf, ...), custom_call_target="tpu_custom_call" | custom-call | tf_op jit(solution)/shard_map/hand_over/pallas_call | solution.py:637

commit v5 on v4

--- a/solution.py
+++ b/solution.py
@@ -193,10 +193,12 @@
     mine = pl.multiple_of(core * HD, HD)
     whole = pl.ds(mine, HD)
     upper, lower = pl.ds(mine, 32), pl.ds(mine + 32, 32)
-    wown = []
-    for w in (wkv, wqo):
+
+    def wfirst(w):
         piece = w.at[y, whole]
-        wown.append((start(piece, piece, up), start(piece, piece, down)))
+        return start(piece, piece, up), start(piece, piece, down)
+
+    wown = [wfirst(wkv)]
     tables = net.group(asked.at[pl.ds(0, PARTS - 1)])
     for q in doms:
         tables.start(req.at[q], asked.at[d], dev(q, x, y))
@@ -240,7 +242,6 @@
 
     mkv = wmiddle(0)
     ffwd = xmiddle(feat_all, fx)
-    mqo = wmiddle(1)
     wlast(0, mkv)
     low4 = (lanes((BLK, 512)) & 127) < HD
 
@@ -271,8 +272,9 @@
     cp.start()
     for c in ffwd:
         c.wait_recv()
+    project_kv(x2)
+    wown.append(wfirst(wqo))
     cx = along_x(cot, cot_all)
-    project_kv(x2)
     cp.wait()
     tp.wait()
     kvs.wait_recv()
@@ -283,9 +285,10 @@
             at = jnp.clip(smem[0, q * 8 + c], 0, NBLK - 1)
             outgoing[k, c] = kv_l[lax.div(at, 4), lax.rem(at, 4)]
         going.start(outgoing.at[k], incoming.at[pl.ds(d * CAP, CAP)], dev(q, x, y))
+    mqo = wmiddle(1)
+    cfwd = xmiddle(cot_all, cx)
     wlast(1, mqo)
     project_qo(x)
-    cfwd = xmiddle(cot_all, cx)
     project_qo(xm)
     project_qo(xp)
     for c in cfwd:

time: 111 us -> 111 us (level)
  no operation moved by 1% of the time
where the time goes in v5:
time: 111 us
  Pallas kernels  109 us (98%)
  between operations  1.29 us (1%)
    pallas_call x1, Pallas kernels, local(): pl.pallas_call(layer_kernel, out_shape=(sds((BLK, WIDTH), BF), sds((BLK,...  108 us

profile of v5, /device:TPU:1, one launch (start us, length us, event | category | flops | bytes accessed | tf_op | source)
XLA Modules:
  0.0 110.7 jit_solution(4957984179280174314)
XLA Ops:
  1.3 107.5 %layer.1 = (bf16[128,1024]{1,0:T(8,128)(2,1)}, bf16[128,1024]{1,0:T(8,128)(2,1)}, f32[64,256]{1,0:T(8,128)}) custom-call(s32[1,16]{1,0:T(1,128)} %source.1, s32[1,16]{1,0:T(1,128)} %target.1, s32[1]{0:T(128)S(6)} %copy.15.count, bf16[128,1024]{1,0:T(8,128)(2,1)} %feat.1, bf16[128,1024]{1,0:T(8,128)(2,1)} %cot.1, bf16[64,1024]{1,0:T(8,128)(2,1)} %bitcast.3, ...), custom_call_target="tpu_custom_call" | custom-call | tf_op jit(solution)/shard_map/layer/pallas_call | solution.py:608
  108.8 1.9 %hand_over.1 = (bf16[128,1024]{1,0:T(8,128)(2,1)}, bf16[128,1024]{1,0:T(8,128)(2,1)}, f32[64,64]{1,0:T(8,128)}, f32[64,64]{1,0:T(8,128)}, f32[64,64]{1,0:T(8,128)}, /*index=5*/f32[64,64]{1,0:T(8,128)}) custom-call(bf16[128,1024]{1,0:T(8,128)(2,1)} %get-tuple-element.9.lo, bf16[128,1024]{1,0:T(8,128)(2,1)} %get-tuple-element.10.gf, ...), custom_call_target="tpu_custom_call" | custom-call | tf_op jit(solution)/shard_map/hand_over/pallas_call | solution.py:640

commit v6 on v5

--- a/solution.py
+++ b/solution.py
@@ -229,15 +229,13 @@
         s3.wait_recv()
 
     def xmiddle(full, halves):
-        (a0, a1), (b0, b1) = halves
+        a0, b0 = halves[0][0], halves[1][0]
         a0.wait_recv()
         p = full.at[xm, pl.ds(0, HD)]
         f1 = start(p, p, right)
         b0.wait_recv()
         p = full.at[xp, pl.ds(HD, HD)]
         f2 = start(p, p, left)
-        a1.wait_recv()
-        b1.wait_recv()
         return f1, f2
 
     mkv = wmiddle(0)
@@ -264,7 +262,9 @@
 
     kvs, qgs = net.group(kv_l.at[pl.ds(0, 3)]), net.group(qg_l.at[pl.ds(0, 3)])
     project_kv(x)
+    fx[0][1].wait_recv()
     project_kv(xm)
+    fx[1][1].wait_recv()
     project_kv(xp)
     tables.wait_recv()
     order_tables(asked, table)
@@ -287,6 +287,8 @@
         going.start(outgoing.at[k], incoming.at[pl.ds(d * CAP, CAP)], dev(q, x, y))
     mqo = wmiddle(1)
     cfwd = xmiddle(cot_all, cx)
+    cx[0][1].wait_recv()
+    cx[1][1].wait_recv()
     wlast(1, mqo)
     project_qo(x)
     project_qo(xm)

time: 111 us -> 110 us (level)
  no operation moved by 1% of the time
where the time goes in v6:
time: 110 us
  Pallas kernels  109 us (99%)
  between operations  1.29 us (1%)
    pallas_call x1, Pallas kernels, local(): pl.pallas_call(layer_kernel, out_shape=(sds((BLK, WIDTH), BF), sds((BLK,...  107 us

profile of v6, /device:TPU:1, one launch (start us, length us, event | category | flops | bytes accessed | tf_op | source)
XLA Modules:
  0.0 110.0 jit_solution(13668426773715183212)
XLA Ops:
  1.3 106.9 %layer.1 = (bf16[128,1024]{1,0:T(8,128)(2,1)}, bf16[128,1024]{1,0:T(8,128)(2,1)}, f32[64,256]{1,0:T(8,128)}) custom-call(s32[1,16]{1,0:T(1,128)} %source.1, s32[1,16]{1,0:T(1,128)} %target.1, s32[1]{0:T(128)S(6)} %copy.15.count, bf16[128,1024]{1,0:T(8,128)(2,1)} %feat.1, bf16[128,1024]{1,0:T(8,128)(2,1)} %cot.1, bf16[64,1024]{1,0:T(8,128)(2,1)} %bitcast.3, ...), custom_call_target="tpu_custom_call" | custom-call | tf_op jit(solution)/shard_map/layer/pallas_call | solution.py:610
  108.2 1.9 %hand_over.1 = (bf16[128,1024]{1,0:T(8,128)(2,1)}, bf16[128,1024]{1,0:T(8,128)(2,1)}, f32[64,64]{1,0:T(8,128)}, f32[64,64]{1,0:T(8,128)}, f32[64,64]{1,0:T(8,128)}, /*index=5*/f32[64,64]{1,0:T(8,128)}) custom-call(bf16[128,1024]{1,0:T(8,128)(2,1)} %get-tuple-element.9.lo, bf16[128,1024]{1,0:T(8,128)(2,1)} %get-tuple-element.10.gf, ...), custom_call_target="tpu_custom_call" | custom-call | tf_op jit(solution)/shard_map/hand_over/pallas_call | solution.py:642

commit v7 on v5

--- a/solution.py
+++ b/solution.py
@@ -529,16 +529,17 @@
         got = returned[jnp.clip(smem[1, k], 0, PARTS * CAP - 1)].astype(F32)
         running = got if k == 0 else got + running * smem[2, k].astype(F32)
         runs[k] = running
-    for s in range(NBLK):
-        more = jnp.where(
-            smem[4, s] > 0,
-            runs[jnp.clip(smem[3, s], 0, CAP * (PARTS - 1) - 1)],
-            jnp.zeros((128, BLK), F32),
-        )
-        gkv[s // 4, s % 4] = jnp.transpose(dkv[s] + more).astype(BF)
     xorder = [(x2, xopp), (xp, right), (xm, left), (x, None)]
     gks = []
     for b, _ in xorder:
+        for h in range(Y):
+            s = h * X + b
+            more = jnp.where(
+                smem[4, s] > 0,
+                runs[jnp.clip(smem[3, s], 0, CAP * (PARTS - 1) - 1)],
+                jnp.zeros((128, BLK), F32),
+            )
+            gkv[h, b] = jnp.transpose(dkv[s] + more).astype(BF)
         c = net.group(g_kv.at[pl.ds(0, 3), b])
         for yy, to in ysteps:
             c.start(gkv.at[yy, b], g_kv.at[y, b], to)

time: 111 us -> 111 us (level)
  no operation moved by 1% of the time
where the time goes in v7:
time: 111 us; the launch traced here: 110 us
  Pallas kernels  109 us (98%)
  between operations  1.29 us (1%)
    pallas_call x1, Pallas kernels, local(): pl.pallas_call(layer_kernel, out_shape=(sds((BLK, WIDTH), BF), sds((BLK,...  107 us

profile of v7, /device:TPU:1, one launch (start us, length us, event | category | flops | bytes accessed | tf_op | source)
XLA Modules:
  0.0 110.5 jit_solution(16463285935875337218)
XLA Ops:
  1.3 107.3 %layer.1 = (bf16[128,1024]{1,0:T(8,128)(2,1)}, bf16[128,1024]{1,0:T(8,128)(2,1)}, f32[64,256]{1,0:T(8,128)}) custom-call(s32[1,16]{1,0:T(1,128)} %source.1, s32[1,16]{1,0:T(1,128)} %target.1, s32[1]{0:T(128)S(6)} %copy.15.count, bf16[128,1024]{1,0:T(8,128)(2,1)} %feat.1, bf16[128,1024]{1,0:T(8,128)(2,1)} %cot.1, bf16[64,1024]{1,0:T(8,128)(2,1)} %bitcast.3, ...), custom_call_target="tpu_custom_call" | custom-call | tf_op jit(solution)/shard_map/layer/pallas_call | solution.py:609
  108.6 1.9 %hand_over.1 = (bf16[128,1024]{1,0:T(8,128)(2,1)}, bf16[128,1024]{1,0:T(8,128)(2,1)}, f32[64,64]{1,0:T(8,128)}, f32[64,64]{1,0:T(8,128)}, f32[64,64]{1,0:T(8,128)}, /*index=5*/f32[64,64]{1,0:T(8,128)}) custom-call(bf16[128,1024]{1,0:T(8,128)(2,1)} %get-tuple-element.9.lo, bf16[128,1024]{1,0:T(8,128)(2,1)} %get-tuple-element.10.gf, ...), custom_call_target="tpu_custom_call" | custom-call | tf_op jit(solution)/shard_map/hand_over/pallas_call | solution.py:641

commit v8 on v7

--- a/solution.py
+++ b/solution.py
@@ -229,15 +229,13 @@
         s3.wait_recv()
 
     def xmiddle(full, halves):
-        (a0, a1), (b0, b1) = halves
+        a0, b0 = halves[0][0], halves[1][0]
         a0.wait_recv()
         p = full.at[xm, pl.ds(0, HD)]
         f1 = start(p, p, right)
         b0.wait_recv()
         p = full.at[xp, pl.ds(HD, HD)]
         f2 = start(p, p, left)
-        a1.wait_recv()
-        b1.wait_recv()
         return f1, f2
 
     mkv = wmiddle(0)
@@ -264,7 +262,9 @@
 
     kvs, qgs = net.group(kv_l.at[pl.ds(0, 3)]), net.group(qg_l.at[pl.ds(0, 3)])
     project_kv(x)
+    fx[0][1].wait_recv()
     project_kv(xm)
+    fx[1][1].wait_recv()
     project_kv(xp)
     tables.wait_recv()
     order_tables(asked, table)
@@ -287,6 +287,8 @@
         going.start(outgoing.at[k], incoming.at[pl.ds(d * CAP, CAP)], dev(q, x, y))
     mqo = wmiddle(1)
     cfwd = xmiddle(cot_all, cx)
+    cx[0][1].wait_recv()
+    cx[1][1].wait_recv()
     wlast(1, mqo)
     project_qo(x)
     project_qo(xm)
@@ -347,7 +349,7 @@
     lax.fori_loop(0, NBLK // 2, forward, 0)
     going.wait_recv()
 
-    batch = 8
+    batch = 16
 
     def extras(g, _):
         ids = [batch * g + i for i in range(batch)]

time: 111 us -> 110 us (level)
  no operation moved by 1% of the time
where the time goes in v8:
time: 110 us
  Pallas kernels  108 us (98%)
  between operations  1.29 us (1%)
    pallas_call x1, Pallas kernels, local(): pl.pallas_call(layer_kernel, out_shape=(sds((BLK, WIDTH), BF), sds((BLK,...  106 us

profile of v8, /device:TPU:1, one launch (start us, length us, event | category | flops | bytes accessed | tf_op | source)
XLA Modules:
  0.0 109.6 jit_solution(14917542913530394635)
XLA Ops:
  1.3 106.4 %layer.1 = (bf16[128,1024]{1,0:T(8,128)(2,1)}, bf16[128,1024]{1,0:T(8,128)(2,1)}, f32[64,256]{1,0:T(8,128)}) custom-call(s32[1,16]{1,0:T(1,128)} %source.1, s32[1,16]{1,0:T(1,128)} %target.1, s32[1]{0:T(128)S(6)} %copy.15.count, bf16[128,1024]{1,0:T(8,128)(2,1)} %feat.1, bf16[128,1024]{1,0:T(8,128)(2,1)} %cot.1, bf16[64,1024]{1,0:T(8,128)(2,1)} %bitcast.3, ...), custom_call_target="tpu_custom_call" | custom-call | tf_op jit(solution)/shard_map/layer/pallas_call | solution.py:611
  107.7 1.9 %hand_over.1 = (bf16[128,1024]{1,0:T(8,128)(2,1)}, bf16[128,1024]{1,0:T(8,128)(2,1)}, f32[64,64]{1,0:T(8,128)}, f32[64,64]{1,0:T(8,128)}, f32[64,64]{1,0:T(8,128)}, /*index=5*/f32[64,64]{1,0:T(8,128)}) custom-call(bf16[128,1024]{1,0:T(8,128)(2,1)} %get-tuple-element.9.lo, bf16[128,1024]{1,0:T(8,128)(2,1)} %get-tuple-element.10.gf, ...), custom_call_target="tpu_custom_call" | custom-call | tf_op jit(solution)/shard_map/hand_over/pallas_call | solution.py:643
